TPU v7x, 256 devices: a whole 4x4x8 slice. The times are simulated.
256 devices in a mesh: dp: 4 (over z_hi, core), section: 16 (over y, z_lo), tensor: 4 (over x).
Axes of the slice: x: 4, y: 4, z: 8 (z_hi: 2, z_lo: 4; z = z_hi * 4 + z_lo), core: 2. Of those that a mesh axis runs over, the one named last changes fastest.
Arguments:
- x_in: bfloat16 [16, 2048, 4096], P('section', ('dp', 'tensor')), may hold values from -6 to 6
- gain: bfloat16 [16, 4096], P('section'), may hold values from 0.5 to 1.5
- weight: bfloat16 [16, 4096, 4096], P('section', 'dp', 'tensor'), may hold values from -0.09375 to 0.09375
- moment_one: bfloat16 [16, 4096, 4096], P('section', 'dp', 'tensor'), may hold values from -0.039794922 to 0.039794922
- moment_two: bfloat16 [16, 4096, 4096], P('section', 'dp', 'tensor'), may hold values from 1.9907951e-05 to 0.00029945374
- cotangent: bfloat16 [16, 2048, 4096], P('section', ('dp', 'tensor')), may hold values from -6 to 6
- preempted: int32 [4, 16], replicated, may hold values from 0 to 1, as said below
Outputs:
- y_out: bfloat16 [16, 2048, 4096], P('section', ('dp', 'tensor'))
- dx_out: bfloat16 [16, 2048, 4096], P('section', ('dp', 'tensor'))
- update: bfloat16 [16, 4096, 4096], P('section', 'dp', 'tensor')
Inputs may be any that keep to these rules, and one draw needn't show every extreme that they name: No two sections of one data group that are neighbours in the loop of 16 sections are both preempted, and data group 0 has at least one preempted section.
All inputs are finite; a program needn't handle non-finite values.
Results may differ from a plain program's by a relative error of at most 0.03.
Values may be sent and summed in bfloat16 or wider, within the bound.
A program may use at most 128 MiB of HBM per device.

v0:
```python
import jax
import jax.numpy as jnp
from jax import lax
from jax.sharding import PartitionSpec as P

EPSILON = 1e-05
BETA_ONE = 0.9
BETA_TWO = 0.95


def from_behind(value, axis, steps):
    count = lax.axis_size(axis)
    pairs = [(source, (source + steps) % count) for source in range(count)]
    return lax.ppermute(value, axis, pairs)


def activate(values):
    return jax.nn.gelu(values, approximate=True)


def normalize(widened, gain_row):
    inverse = lax.rsqrt(jnp.mean(widened * widened, axis=-1, keepdims=True) + EPSILON)
    return widened * inverse * gain_row.astype(jnp.float32)


def forward_part(inputs, gain_row, weight_cols):
    widened = inputs.astype(jnp.float32)
    normed_local = normalize(widened, gain_row).astype(jnp.bfloat16)
    normed_all = lax.all_gather(normed_local, "tensor", axis=0, tiled=True)
    hidden = jnp.dot(normed_all, weight_cols, preferred_element_type=jnp.float32)
    branch = activate(hidden).astype(jnp.bfloat16)
    branch_rows = lax.all_to_all(branch, "tensor", split_axis=0, concat_axis=1, tiled=True)
    output = (widened + branch_rows.astype(jnp.float32)).astype(jnp.bfloat16)
    return (output, normed_all, hidden)


def backward_part(incoming, inputs, gain_row, weight_cols, hidden):
    upstream = incoming.astype(jnp.float32)
    incoming_cols = lax.all_to_all(incoming, "tensor", split_axis=1, concat_axis=0, tiled=True)
    hidden_grad = jax.vjp(activate, hidden)[1](incoming_cols.astype(jnp.float32))[0].astype(
        jnp.bfloat16
    )
    normed_grad = lax.psum_scatter(
        lax.dot_general(
            hidden_grad, weight_cols, (((1,), (1,)), ((), ())), preferred_element_type=jnp.float32
        ).astype(jnp.bfloat16),
        "tensor",
        scatter_dimension=0,
        tiled=True,
    ).astype(jnp.float32)
    input_grad = jax.vjp(lambda values: normalize(values, gain_row), inputs.astype(jnp.float32))[1](
        normed_grad
    )[0]
    return (upstream + input_grad, hidden_grad)


def body(x_in, gain, weight, moment_one, moment_two, cotangent, preempted):
    section_here = lax.axis_index("section")
    section_count = lax.axis_size("section")
    group_here = lax.axis_index("dp")
    flag_row = lax.dynamic_index_in_dim(preempted, group_here, 0, keepdims=False)
    flag_self = lax.dynamic_index_in_dim(flag_row, section_here, 0, keepdims=False) == 1
    next_index = (section_here + 1) % section_count
    flag_next = lax.dynamic_index_in_dim(flag_row, next_index, 0, keepdims=False) == 1
    inputs = x_in[0]
    upstream = cotangent[0]
    gain_row = gain[0]
    weight_shard = weight[0]
    weight_cols = lax.all_gather(weight_shard, "dp", axis=0, tiled=True)
    first_out, first_normed, first_hidden = forward_part(inputs, gain_row, weight_cols)
    next_weight, next_gain = from_behind((weight_shard, gain_row), "section", -1)
    next_cols = lax.all_gather(next_weight, "dp", axis=0, tiled=True)
    succ_out, succ_normed, succ_hidden = forward_part(first_out, next_gain, next_cols)
    other_out, prior_rows, other_normed, other_hidden = (
        from_behind(succ_out, "section", 1),
        from_behind(first_out, "section", 1),
        from_behind(succ_normed, "section", 1),
        from_behind(succ_hidden.astype(jnp.bfloat16), "section", 1).astype(succ_hidden.dtype),
    )
    section_in = jnp.where(flag_self, prior_rows, inputs)
    section_out = jnp.where(flag_self, other_out, first_out)
    normed_all = jnp.where(flag_self, other_normed, first_normed)
    hidden = jnp.where(flag_self, other_hidden, first_hidden)
    early_grad, unused_grad = backward_part(upstream, section_in, gain_row, weight_cols, hidden)
    received = from_behind(early_grad.astype(jnp.bfloat16), "section", -1)
    summed = (upstream.astype(jnp.float32) + received.astype(jnp.float32)).astype(jnp.bfloat16)
    incoming = jnp.where(flag_next, summed, upstream)
    input_grad, hidden_grad = backward_part(incoming, section_in, gain_row, weight_cols, hidden)
    carried = input_grad.astype(jnp.bfloat16)
    grad_in = jnp.where(flag_self, jnp.zeros_like(carried), carried)
    scale = 1.0 / (lax.axis_size("dp") * inputs.shape[0] * lax.axis_size("tensor"))
    total = lax.psum_scatter(
        (
            lax.dot_general(
                normed_all,
                hidden_grad,
                (((0,), (0,)), ((), ())),
                preferred_element_type=jnp.float32,
            )
            * scale
        ).astype(jnp.bfloat16),
        "dp",
        scatter_dimension=0,
        tiled=True,
    ).astype(jnp.float32)
    first_moment = BETA_ONE * moment_one[0].astype(jnp.float32) + (1.0 - BETA_ONE) * total
    second_moment = BETA_TWO * moment_two[0].astype(jnp.float32) + (1.0 - BETA_TWO) * total * total
    step_dir = (first_moment / (jnp.sqrt(second_moment) + 1e-08)).astype(jnp.bfloat16)
    return (section_out[None], grad_in[None], step_dir[None])


def solution(mesh):
    placed = (
        P("section", ("dp", "tensor"), None),
        P("section", None),
        P("section", "dp", "tensor"),
        P("section", "dp", "tensor"),
        P("section", "dp", "tensor"),
        P("section", ("dp", "tensor"), None),
        P(),
    )
    return jax.shard_map(
        body,
        mesh=mesh,
        in_specs=placed,
        out_specs=(
            P("section", ("dp", "tensor"), None),
            P("section", ("dp", "tensor"), None),
            P("section", "dp", "tensor"),
        ),
        check_vma=False,
    )
```

profile of v0, /device:TPU:1, one launch (start us, length us, event | category | flops | bytes accessed | tf_op | source)
XLA Modules:
  0.0 762.1 jit_solution(1832808648149123732)
XLA Ops:
  7.2 0.8 reduce
  8.0 1.5 fusion.26
  9.5 2.5 fusion.28
  12.1 0.7 all-gather.12.cloned.1.call-update
  12.9 0.8 copy-done.6
  13.6 7.6 %collective-permute-start.1 = (bf16[1024,1024]{1,0:T(8,128)(2,1)S(1)}, bf16[1024,1024]{1,0:T(8,128)(2,1)}, u32[]{:S(2)}, u32[]{:S(2)}) collective-permute-start(bf16[1024,1024]{1,0:T(8,128)(2,1)S(1)} %bitcast.98), channel_id=1, source_target_pairs={{0,60},{4,0},{8,4},{12,8},{16,12},{20,16},{24,20},{28,24},{32,28},... | collective-permute-start | bytes 6291464 | tf_op jit(solution)/shard_map/ppermute | solution.py:14
  21.3 44.3 %collective-permute-done.1 = bf16[1024,1024]{1,0:T(8,128)(2,1)} collective-permute-done((bf16[1024,1024]{1,0:T(8,128)(2,1)S(1)}, bf16[1024,1024]{1,0:T(8,128)(2,1)}, u32[]{:S(2)}, u32[]{:S(2)}) %collective-permute-start.1) | collective-permute-done | bytes 2097184 | tf_op jit(solution)/shard_map/ppermute | solution.py:14
  65.6 1.2 all-gather.6.cloned.1.call-done
  66.8 116.2 %all-gather.12.cloned.1.call-done = bf16[1,4096,1024]{2,1,0:T(8,128)(2,1)} async-done(((bf16[1,1024,1024]{2,1,0:T(8,128)(2,1)}), bf16[1,4096,1024]{2,1,0:T(8,128)(2,1)}) %all-gather.12.cloned.1.call-update) | async-done | bytes 8388624 | tf_op jit(solution)/shard_map/all_gather | solution.py:69
  183.0 11.1 %fusion.37 = (bf16[512,1024]{1,0:T(8,128)(2,1)}, f32[512,1024]{1,0:T(8,128)}) fusion(bf16[512,4096]{1,0:T(8,128)(2,1)} %all-gather.6.cloned.1.call-done, bf16[1,4096,1024]{2,1,0:T(8,128)(2,1)} %all-gather.12.cloned.1.call-done), kind=kOutput, calls=%fused_computation.55 | convolution fusion | flops 4299685888 | bytes 15728640 | tf_op jit(solution)/shard_map/dot_general | solution.py:30
  194.1 4.0 all-to-all-start
  198.1 4.2 collective-permute-done
  202.3 10.5 %all-to-all-done = bf16[4,128,1024]{2,1,0:T(8,128)(2,1)S(1)} async-done(((bf16[4,128,1024]{2,1,0:T(8,128)(2,1)}), bf16[4,128,1024]{2,1,0:T(8,128)(2,1)S(1)}, u32[]{:S(2)}, u32[]{:S(2)}) %all-to-all-start) | async-done | bytes 1048608 | tf_op jit(solution)/shard_map/all_to_all | solution.py:32
  213.3 1.0 copy-done
  214.3 0.4 fusion.38
  214.8 1.3 fusion.40
  216.1 78.4 %all-gather.10.cloned.1.call-done = bf16[4096,1024]{1,0:T(8,128)(2,1)} async-done(((bf16[1024,1024]{1,0:T(8,128)(2,1)}), bf16[4096,1024]{1,0:T(8,128)(2,1)}) %all-gather.10.cloned.1.call-update) | async-done | bytes 8388624 | tf_op jit(solution)/shard_map/all_gather | solution.py:72
  294.5 48.8 %all-gather.8.cloned.1.call-done = bf16[512,4096]{1,0:T(8,128)(2,1)} async-done(((bf16[128,4096]{1,0:T(8,128)(2,1)}), bf16[512,4096]{1,0:T(8,128)(2,1)}) %all-gather.8.cloned.1.call-update) | async-done | bytes 4194320 | tf_op jit(solution)/shard_map/all_gather | solution.py:29
  343.3 10.9 %fusion.71 = (bf16[512,1024]{1,0:T(8,128)(2,1)}, bf16[512,1024]{1,0:T(8,128)(2,1)}) fusion(bf16[512,4096]{1,0:T(8,128)(2,1)} %all-gather.8.cloned.1.call-done, bf16[4096,1024]{1,0:T(8,128)(2,1)} %all-gather.10.cloned.1.call-done), kind=kOutput, calls=%fused_computation.107 | convolution fusion | flops 4300210176 | bytes 14680064 | tf_op jit(solution)/shard_map/dot_general | solution.py:30
  354.1 1.3 collective-permute-start.3
  355.4 1.6 all_to_all.44
  357.0 2.5 copy.12
  359.6 3.5 all-to-all-start.2
  363.2 0.7 fusion.72
  364.5 12.9 %all-to-all-done.2 = bf16[128,4,1024]{2,0,1:T(8,128)(2,1)S(1)} async-done(((bf16[128,4,1024]{2,0,1:T(8,128)(2,1)}), bf16[128,4,1024]{2,0,1:T(8,128)(2,1)S(1)}, u32[]{:S(2)}, u32[]{:S(2)}) %all-to-all-start.2) | async-done | bytes 1048608 | tf_op jit(solution)/shard_map/all_to_all | solution.py:39
  377.3 5.2 collective-permute-done.3
  382.5 3.5 fusion.62
  386.0 9.6 %fusion.6 = bf16[512,4096]{1,0:T(8,128)(2,1)} fusion(bf16[512,1024]{1,0:T(8,128)(2,1)S(1)} %fusion.62, bf16[1,4096,1024]{2,1,0:T(8,128)(2,1)} %all-gather.12.cloned.1.call-done), kind=kOutput, calls=%fused_computation.8 | convolution fusion | flops 4297064448 | bytes 13631488 | tf_op jit(solution)/shard_map/dot_general | solution.py:44
  395.8 27.2 %collective-permute-done.4 = bf16[128,4096]{1,0:T(8,128)(2,1)} collective-permute-done((bf16[128,4096]{1,0:T(8,128)(2,1)S(1)}, bf16[128,4096]{1,0:T(8,128)(2,1)}, u32[]{:S(2)}, u32[]{:S(2)}) %collective-permute-start.4) | collective-permute-done | bytes 1048608 | tf_op jit(solution)/shard_map/ppermute | solution.py:14
  423.0 22.1 %reduce-scatter.4.cloned.1.call-done = bf16[128,4096]{1,0:T(8,128)(2,1)} async-done(((bf16[512,4096]{1,0:T(8,128)(2,1)}), bf16[128,4096]{1,0:T(8,128)(2,1)}) %reduce-scatter.4.cloned.1.call-update) | async-done | bytes 1048592 | tf_op jit(solution)/shard_map/reduce_scatter | solution.py:43
  445.1 2.1 fusion.52
  447.2 2.1 fusion.20
  449.3 5.8 collective-permute-start.5
  455.8 21.2 %collective-permute-done.5 = bf16[128,4096]{1,0:T(8,128)(2,1)S(1)} collective-permute-done((bf16[128,4096]{1,0:T(8,128)(2,1)S(1)}, bf16[128,4096]{1,0:T(8,128)(2,1)S(1)}, u32[]{:S(2)}, u32[]{:S(2)}) %collective-permute-start.5) | collective-permute-done | bytes 1048608 | tf_op jit(solution)/shard_map/ppermute | solution.py:14
  477.4 16.1 %all_to_all.52 = bf16[128,4,1024]{2,0,1:T(8,128)(2,1)S(1)} all-to-all(bf16[128,4,1024]{2,0,1:T(8,128)(2,1)S(1)} %bitcast.97), channel_id=1, replica_groups=mesh['dp'=4,'section'=16,'tensor'=4] {'tensor'}, dimensions={1} | all-to-all | bytes 2097152 | tf_op jit(solution)/shard_map/all_to_all | solution.py:39
  493.5 2.9 fusion.57
  496.4 1.0 copy-done.7
  497.4 9.6 %fusion.9 = bf16[512,4096]{1,0:T(8,128)(2,1)} fusion(bf16[512,1024]{1,0:T(8,128)(2,1)S(1)} %fusion.57, bf16[1,4096,1024]{2,1,0:T(8,128)(2,1)} %all-gather.12.cloned.1.call-done), kind=kOutput, calls=%fused_computation.9 | convolution fusion | flops 4297064448 | bytes 13631488 | tf_op jit(solution)/shard_map/dot_general | solution.py:44
  507.1 94.7 %collective-permute-done.6 = bf16[512,4096]{1,0:T(8,128)(2,1)S(1)} collective-permute-done((bf16[512,4096]{1,0:T(8,128)(2,1)}, bf16[512,4096]{1,0:T(8,128)(2,1)S(1)}, u32[]{:S(2)}, u32[]{:S(2)}) %collective-permute-start.6) | collective-permute-done | bytes 4194336 | tf_op jit(solution)/shard_map/ppermute | solution.py:14
  601.8 10.6 %multiply_convert_fusion = bf16[4096,1024]{1,0:T(8,128)(2,1)} fusion(bf16[512,1024]{1,0:T(8,128)(2,1)} %copy-done.7, bf16[512,4096]{1,0:T(8,128)(2,1)S(1)} %collective-permute-done.6, bf16[512,4096]{1,0:T(8,128)(2,1)} %all-gather.6.cloned.1.call-done, pred[]{:T(512)} %bitcast), kind=kOutput, calls=%fused_computation | convolution fusion | flops 4305453056 | bytes 17825792 | tf_op jit(solution)/shard_map/dot_general | solution.py:94
  612.4 15.4 %all_to_all.53 = bf16[4,128,1024]{2,1,0:T(8,128)(2,1)S(1)} all-to-all(bf16[4,128,1024]{2,1,0:T(8,128)(2,1)} %bitcast.99), channel_id=1, replica_groups=mesh['dp'=4,'section'=16,'tensor'=4] {'tensor'}, dimensions={0} | all-to-all | bytes 2097152 | tf_op jit(solution)/shard_map/all_to_all | solution.py:32
  628.6 0.3 collective-permute-start.2
  628.9 28.3 %collective-permute-done.2 = bf16[128,4096]{1,0:T(8,128)(2,1)S(1)} collective-permute-done((bf16[128,4096]{1,0:T(8,128)(2,1)S(1)}, bf16[128,4096]{1,0:T(8,128)(2,1)S(1)}, u32[]{:S(2)}, u32[]{:S(2)}) %collective-permute-start.2) | collective-permute-done | bytes 1048608 | tf_op jit(solution)/shard_map/ppermute | solution.py:14
  657.2 1.1 select_bitcast_fusion
  658.3 1.7 fusion.54
  660.1 1.8 fusion.68
  661.9 86.4 %reduce-scatter.8.cloned.1.call-done = bf16[1024,1024]{1,0:T(8,128)(2,1)} async-done(((bf16[4096,1024]{1,0:T(8,128)(2,1)}), bf16[1024,1024]{1,0:T(8,128)(2,1)}) %reduce-scatter.8.cloned.1.call-update) | async-done | bytes 2097168 | tf_op jit(solution)/shard_map/reduce_scatter | solution.py:92
  748.3 7.0 fusion.65
  (45 shorter events, 2.2 us)
Async XLA Ops:
  7.2 59.7 %all-gather.6.cloned.1.call-start = ((), (), s32[]{:S(2)}) async-start(), calls=%async_computation.7 | async-start | bytes 5242880 | tf_op jit(solution)/shard_map/all_gather | solution.py:29
  12.0 1.6 copy-start.6
  12.1 170.9 %all-gather.12.cloned.1.call-start = ((), (), s32[]{:S(2)}) async-start(), calls=%async_computation.13 | async-start | bytes 10485760 | tf_op jit(solution)/shard_map/all_gather | solution.py:69
  12.8 281.7 %all-gather.10.cloned.1.call-start = ((), (), s32[]{:S(2)}) async-start(), calls=%async_computation.9 | async-start | bytes 10485760 | tf_op jit(solution)/shard_map/all_gather | solution.py:72
  13.6 51.9 %collective-permute-start.1 = (bf16[1024,1024]{1,0:T(8,128)(2,1)S(1)}, bf16[1024,1024]{1,0:T(8,128)(2,1)}, u32[]{:S(2)}, u32[]{:S(2)}) collective-permute-start(bf16[1024,1024]{1,0:T(8,128)(2,1)S(1)} %bitcast.98), channel_id=1, source_target_pairs={{0,60},{4,0},{8,4},{12,8},{16,12},{20,16},{24,20},{28,24},{32,28},... | collective-permute-start | bytes 6291464 | tf_op jit(solution)/shard_map/ppermute | solution.py:14
  194.1 18.7 %all-to-all-start = ((bf16[4,128,1024]{2,1,0:T(8,128)(2,1)}), bf16[4,128,1024]{2,1,0:T(8,128)(2,1)S(1)}, u32[]{:S(2)}, u32[]{:S(2)}) async-start(bf16[4,128,1024]{2,1,0:T(8,128)(2,1)} %bitcast.3), calls=%async_computation | async-start | bytes 2097152 | tf_op jit(solution)/shard_map/all_to_all | solution.py:32
  198.1 145.2 %all-gather.8.cloned.1.call-start = ((), (), s32[]{:S(2)}) async-start(), calls=%async_computation.8 | async-start | bytes 5242880 | tf_op jit(solution)/shard_map/all_gather | solution.py:29
  198.1 4.3 collective-permute-start
  213.1 1.2 copy-start
  216.1 139.3 %copy-start.1 = (bf16[1,128,4096]{2,1,0:T(8,128)(2,1)S(1)}, bf16[1,128,4096]{2,1,0:T(8,128)(2,1)}, u32[]{:S(2)}) copy-start(bf16[1,128,4096]{2,1,0:T(8,128)(2,1)} %param.12) | copy-start | bytes 3145732
  354.1 28.4 %collective-permute-start.3 = (bf16[512,1024]{1,0:T(8,128)(2,1)}, bf16[512,1024]{1,0:T(8,128)(2,1)}, u32[]{:S(2)}, u32[]{:S(2)}) collective-permute-start(bf16[512,1024]{1,0:T(8,128)(2,1)} %get-tuple-element.10), channel_id=1, source_target_pairs={{0,4},{4,8},{8,12},{12,16},{16,20},{20,24},{24,28},{28,32},{32,36}... | collective-permute-start | bytes 3145736 | tf_op jit(solution)/shard_map/ppermute | solution.py:14
  357.0 6.1 copy-start.8
  359.6 17.8 %all-to-all-start.2 = ((bf16[128,4,1024]{2,0,1:T(8,128)(2,1)}), bf16[128,4,1024]{2,0,1:T(8,128)(2,1)S(1)}, u32[]{:S(2)}, u32[]{:S(2)}) async-start(bf16[128,4,1024]{2,0,1:T(8,128)(2,1)} %copy.12), calls=%async_computation.2 | async-start | bytes 2097152 | tf_op jit(solution)/shard_map/all_to_all | solution.py:39
  363.1 82.0 %reduce-scatter.4.cloned.1.call-start = ((), (), s32[]{:S(2)}) async-start(), calls=%async_computation.10 | async-start | bytes 5242880 | tf_op jit(solution)/shard_map/reduce_scatter | solution.py:43
  395.6 262.7 %reduce-scatter.6.cloned.1.call-start = ((), (), s32[]{:S(2)}) async-start(), calls=%async_computation.11 | async-start | bytes 5242880 | tf_op jit(solution)/shard_map/reduce_scatter | solution.py:43
  395.7 27.3 %collective-permute-start.4 = (bf16[128,4096]{1,0:T(8,128)(2,1)S(1)}, bf16[128,4096]{1,0:T(8,128)(2,1)}, u32[]{:S(2)}, u32[]{:S(2)}) collective-permute-start(bf16[128,4096]{1,0:T(8,128)(2,1)S(1)} %get-tuple-element.9), channel_id=1, source_target_pairs={{0,4},{4,8},{8,12},{12,16},{16,20},{20,24},{24,28},{28,32},{32,36}... | collective-permute-start | bytes 3145736 | tf_op jit(solution)/shard_map/ppermute | solution.py:14
  445.1 2.1 copy-start.4
  447.2 29.8 %copy-start.2 = (bf16[1,128,4096]{2,1,0:T(8,128)(2,1)S(1)}, bf16[1,128,4096]{2,1,0:T(8,128)(2,1)}, u32[]{:S(2)}) copy-start(bf16[1,128,4096]{2,1,0:T(8,128)(2,1)} %param.12) | copy-start | bytes 3145732
  449.3 27.7 %collective-permute-start.5 = (bf16[128,4096]{1,0:T(8,128)(2,1)S(1)}, bf16[128,4096]{1,0:T(8,128)(2,1)S(1)}, u32[]{:S(2)}, u32[]{:S(2)}) collective-permute-start(bf16[128,4096]{1,0:T(8,128)(2,1)S(1)} %fusion.20), channel_id=1, source_target_pairs={{0,60},{4,0},{8,4},{12,8},{16,12},{20,16},{24,20},{28,24},{32,28},... | collective-permute-start | bytes 3145736 | tf_op jit(solution)/shard_map/ppermute | solution.py:14
  477.3 16.2 %copy-start.3 = (f32[512,1024]{1,0:T(8,128)S(1)}, f32[512,1024]{1,0:T(8,128)}, u32[]{:S(2)}) copy-start(f32[512,1024]{1,0:T(8,128)} %get-tuple-element.16) | copy-start | bytes 6291460
  496.4 1.0 copy-start.7
  507.0 241.3 %reduce-scatter.8.cloned.1.call-start = ((), (), s32[]{:S(2)}) async-start(), calls=%async_computation.12 | async-start | bytes 10485760 | tf_op jit(solution)/shard_map/reduce_scatter | solution.py:92
  507.0 94.8 %collective-permute-start.6 = (bf16[512,4096]{1,0:T(8,128)(2,1)}, bf16[512,4096]{1,0:T(8,128)(2,1)S(1)}, u32[]{:S(2)}, u32[]{:S(2)}) collective-permute-start(bf16[512,4096]{1,0:T(8,128)(2,1)} %all-gather.8.cloned.1.call-done), channel_id=1, source_target_pairs={{0,4},{4,8},{8,12},{12,16},{16,20},{20,24},{24,28},{28,32},{32,36}... | collective-permute-start | bytes 12582920 | tf_op jit(solution)/shard_map/ppermute | solution.py:14
  628.6 28.6 %collective-permute-start.2 = (bf16[128,4096]{1,0:T(8,128)(2,1)S(1)}, bf16[128,4096]{1,0:T(8,128)(2,1)S(1)}, u32[]{:S(2)}, u32[]{:S(2)}) collective-permute-start(bf16[128,4096]{1,0:T(8,128)(2,1)S(1)} %fusion.41), channel_id=1, source_target_pairs={{0,4},{4,8},{8,12},{12,16},{16,20},{20,24},{24,28},{28,32},{32,36}... | collective-permute-start | bytes 3145736 | tf_op jit(solution)/shard_map/ppermute | solution.py:14
  658.3 1.7 copy-start.5
Sparse Core Ops, SparseCore 0:
  12.2 54.5 all-gather.5
  68.6 114.3 all-gather.11
  184.8 109.6 all-gather.9
  296.7 46.4 all-gather.7
  395.8 49.2 reduce-scatter.3
  507.1 48.9 reduce-scatter.5
  612.5 135.7 reduce-scatter.7
where the time goes:
time: 763 us; the launch traced here: 762 us
  waiting for transfers between devices  602 us (79%)
  matrix products  51.8 us (7%)
  blocking collectives  31.5 us (4%)
  other arithmetic  29.7 us (4%)
  starting transfers between devices  23 us (3%)
  between operations  15.7 us (2%)
  local copies, waits for them, and re-layouts  8.1 us (1%)
    ppermute x7, waiting for transfers between devices, from_behind(): return lax.ppermute(value, axis, pairs)  225 us
    all_gather x1, waiting for transfers between devices, body(): weight_cols = lax.all_gather(weight_shard, 'dp', axis=0, tiled=True)  116 us
    reduce_scatter x1, waiting for transfers between devices, body(): lax.psum_scatter((lax.dot_general(normed_all, hidden_grad, (((0,), (0,)),...  86.4 us
    all_gather x1, waiting for transfers between devices, body(): next_cols = lax.all_gather(next_weight, 'dp', axis=0, tiled=True)  78.4 us
    all_gather x2, waiting for transfers between devices, forward_part(): normed_all = lax.all_gather(normed_local, 'tensor', axis=0, tiled=True)  50 us
    reduce_scatter x2, waiting for transfers between devices, backward_part(): lax.psum_scatter(lax.dot_general(hidden_grad, weight_cols, (((1,), (1,)),...  22.1 us
    dot_general x2, matrix products, forward_part(): jnp.dot(normed_all, weight_cols, preferred_element_type=jnp.float32)  22 us
    dot_general x2, matrix products, backward_part(): lax.dot_general(hidden_grad, weight_cols, (((1,), (1,)), ((), ())), prefe...  19.2 us
  transfers between devices with their start and end apart: 16, of which 15 were waited for; matrix products, arithmetic and copies ran while one was open for 4% of the time, Pallas kernels for 0%

commit v1 on v0

--- a/solution.py
+++ b/solution.py
@@ -67,20 +67,10 @@
     gain_row = gain[0]
     weight_shard = weight[0]
     weight_cols = lax.all_gather(weight_shard, "dp", axis=0, tiled=True)
-    first_out, first_normed, first_hidden = forward_part(inputs, gain_row, weight_cols)
-    next_weight, next_gain = from_behind((weight_shard, gain_row), "section", -1)
-    next_cols = lax.all_gather(next_weight, "dp", axis=0, tiled=True)
-    succ_out, succ_normed, succ_hidden = forward_part(first_out, next_gain, next_cols)
-    other_out, prior_rows, other_normed, other_hidden = (
-        from_behind(succ_out, "section", 1),
-        from_behind(first_out, "section", 1),
-        from_behind(succ_normed, "section", 1),
-        from_behind(succ_hidden.astype(jnp.bfloat16), "section", 1).astype(succ_hidden.dtype),
-    )
+    first_out, _, _ = forward_part(inputs, gain_row, weight_cols)
+    prior_rows = from_behind(first_out, "section", 1)
     section_in = jnp.where(flag_self, prior_rows, inputs)
-    section_out = jnp.where(flag_self, other_out, first_out)
-    normed_all = jnp.where(flag_self, other_normed, first_normed)
-    hidden = jnp.where(flag_self, other_hidden, first_hidden)
+    section_out, normed_all, hidden = forward_part(section_in, gain_row, weight_cols)
     early_grad, unused_grad = backward_part(upstream, section_in, gain_row, weight_cols, hidden)
     received = from_behind(early_grad.astype(jnp.bfloat16), "section", -1)
     summed = (upstream.astype(jnp.float32) + received.astype(jnp.float32)).astype(jnp.bfloat16)

time: 763 us -> 626 us (0.82)
  waiting for transfers between devices: 602 us -> 442 us
  blocking collectives: 31.5 us -> 81.8 us
  starting transfers between devices: 23 us -> 5.83 us
    ppermute x7 -> x2, waiting for transfers between devices: 225 us -> 46.8 us  [from_behind(): return lax.ppermute(value, axis, pairs)]
    all_gather x1 -> x0, waiting for transfers between devices: 78.4 us -> none  [body(): next_cols = lax.all_gather(next_weight, 'dp', axis=0, tiled=True)]
    reduce_scatter x1, waiting for transfers between devices: 86.4 us -> 129 us  [body(): lax.psum_scatter((lax.dot_general(normed_all, hidden_grad, (((0,), (0,)),...]
    reduce_scatter x2, waiting for transfers between devices: 22.1 us -> 63.1 us  [backward_part(): lax.psum_scatter(lax.dot_general(hidden_grad, weight_cols, (((1,), (1,)),...]
    all_gather x2, waiting for transfers between devices: 50 us -> 86.4 us  [forward_part(): normed_all = lax.all_gather(normed_local, 'tensor', axis=0, tiled=True)]
    all_to_all x1 -> x2, blocking collectives: 15.4 us -> 46.3 us  [forward_part(): lax.all_to_all(branch, 'tensor', split_axis=0, concat_axis=1, tiled=True)]
    all_to_all x2 -> x0, waiting for transfers between devices: 23.4 us -> none  [the longest x1 12.9 us: backward_part(): lax.all_to_all(incoming, 'tensor', split_axis=1, concat_axis=0, tiled=True)]
    all_to_all x1 -> x2, blocking collectives: 16.1 us -> 35.5 us  [backward_part(): lax.all_to_all(incoming, 'tensor', split_axis=1, concat_axis=0, tiled=True)]
  transfers between devices with their start and end apart: 16 -> 8, of which waited for: 15 -> 8; matrix products, arithmetic and copies ran while one was open for 4% -> 3% of each run, Pallas kernels for 0% -> 0%
where the time goes in v1:
time: 626 us
  waiting for transfers between devices  442 us (71%)
  blocking collectives  81.8 us (13%)
  matrix products  50.5 us (8%)
  other arithmetic  23.8 us (4%)
  between operations  15.6 us (2%)
    reduce_scatter x1, waiting for transfers between devices, body(): lax.psum_scatter((lax.dot_general(normed_all, hidden_grad, (((0,), (0,)),...  129 us
    all_gather x1, waiting for transfers between devices, body(): weight_cols = lax.all_gather(weight_shard, 'dp', axis=0, tiled=True)  116 us
    all_gather x2, waiting for transfers between devices, forward_part(): normed_all = lax.all_gather(normed_local, 'tensor', axis=0, tiled=True)  86.4 us
    reduce_scatter x2, waiting for transfers between devices, backward_part(): lax.psum_scatter(lax.dot_general(hidden_grad, weight_cols, (((1,), (1,)),...  63.1 us
    ppermute x2, waiting for transfers between devices, from_behind(): return lax.ppermute(value, axis, pairs)  46.8 us
    all_to_all x2, blocking collectives, forward_part(): lax.all_to_all(branch, 'tensor', split_axis=0, concat_axis=1, tiled=True)  46.3 us
    all_to_all x2, blocking collectives, backward_part(): lax.all_to_all(incoming, 'tensor', split_axis=1, concat_axis=0, tiled=True)  35.5 us
    dot_general x2, matrix products, forward_part(): jnp.dot(normed_all, weight_cols, preferred_element_type=jnp.float32)  21.2 us
  transfers between devices with their start and end apart: 8, of which 8 were waited for; matrix products, arithmetic and copies ran while one was open for 3% of the time, Pallas kernels for 0%

profile of v1, /device:TPU:1, one launch (start us, length us, event | category | flops | bytes accessed | tf_op | source)
XLA Modules:
  0.0 625.6 jit_solution(12798719855050187507)
XLA Ops:
  7.2 1.5 fusion.26
  8.7 0.7 mul.283
  9.5 2.5 fusion.28
  12.0 0.0 all-gather.9.cloned.1.call-start
  12.1 0.7 all-gather.9.cloned.1.call-update
  12.8 54.0 %all-gather.5.cloned.1.call-done = bf16[512,4096]{1,0:T(8,128)(2,1)} async-done(((bf16[128,4096]{1,0:T(8,128)(2,1)}), bf16[512,4096]{1,0:T(8,128)(2,1)}) %all-gather.5.cloned.1.call-update) | async-done | bytes 4194320 | tf_op jit(solution)/shard_map/all_gather | solution.py:29
  66.8 116.2 %all-gather.9.cloned.1.call-done = bf16[1,4096,1024]{2,1,0:T(8,128)(2,1)} async-done(((bf16[1,1024,1024]{2,1,0:T(8,128)(2,1)}), bf16[1,4096,1024]{2,1,0:T(8,128)(2,1)}) %all-gather.9.cloned.1.call-update) | async-done | bytes 8388624 | tf_op jit(solution)/shard_map/all_gather | solution.py:69
  183.0 9.5 %fusion.37 = bf16[512,1024]{1,0:T(8,128)(2,1)S(1)} fusion(bf16[512,4096]{1,0:T(8,128)(2,1)} %all-gather.5.cloned.1.call-done, bf16[1,4096,1024]{2,1,0:T(8,128)(2,1)} %all-gather.9.cloned.1.call-done), kind=kOutput, calls=%fused_computation.53 | convolution fusion | flops 4299685888 | bytes 13631488 | tf_op jit(solution)/shard_map/dot_general | solution.py:30
  192.5 18.4 %all_to_all.52 = bf16[4,128,1024]{2,1,0:T(8,128)(2,1)S(1)} all-to-all(bf16[4,128,1024]{2,1,0:T(8,128)(2,1)S(1)} %bitcast.102), channel_id=1, replica_groups=mesh['dp'=4,'section'=16,'tensor'=4] {'tensor'}, dimensions={0} | all-to-all | bytes 2097152 | tf_op jit(solution)/shard_map/all_to_all | solution.py:32
  210.9 0.2 convert_bitcast_fusion.1
  211.2 0.2 copy.15
  211.4 1.0 copy-done
  212.4 0.3 fusion.29
  212.7 0.1 collective-permute-start
  212.8 0.3 copy-done.6
  213.1 0.6 fusion.64
  214.3 25.6 %collective-permute-done = bf16[128,4096]{1,0:T(8,128)(2,1)S(1)} collective-permute-done((bf16[128,4096]{1,0:T(8,128)(2,1)S(1)}, bf16[128,4096]{1,0:T(8,128)(2,1)S(1)}, u32[]{:S(2)}, u32[]{:S(2)}) %collective-permute-start) | collective-permute-done | bytes 1048608 | tf_op jit(solution)/shard_map/ppermute | solution.py:14
  239.9 0.5 fusion.40
  240.4 1.3 fusion.42
  241.7 0.0 reduce-scatter.4.cloned.1.call-start
  241.8 0.8 all_to_all.44
  242.6 0.3 copy.12
  242.9 19.4 %all_to_all.53 = bf16[128,4,1024]{2,0,1:T(8,128)(2,1)S(1)} all-to-all(bf16[128,4,1024]{2,0,1:T(8,128)(2,1)S(1)} %copy.12), channel_id=1, replica_groups=mesh['dp'=4,'section'=16,'tensor'=4] {'tensor'}, dimensions={1} | all-to-all | bytes 2097152 | tf_op jit(solution)/shard_map/all_to_all | solution.py:39
  262.3 32.4 %all-gather.7.cloned.1.call-done = bf16[512,4096]{1,0:T(8,128)(2,1)} async-done(((bf16[128,4096]{1,0:T(8,128)(2,1)}), bf16[512,4096]{1,0:T(8,128)(2,1)}) %all-gather.7.cloned.1.call-update) | async-done | bytes 4194320 | tf_op jit(solution)/shard_map/all_gather | solution.py:29
  294.8 11.6 %fusion.53 = (bf16[512,1024]{1,0:T(8,128)(2,1)S(1)}, f32[512,1024]{1,0:T(8,128)}) fusion(bf16[128,4,1024]{2,0,1:T(8,128)(2,1)S(1)} %all_to_all.53, bf16[512,4096]{1,0:T(8,128)(2,1)} %all-gather.7.cloned.1.call-done, bf16[1,4096,1024]{2,1,0:T(8,128)(2,1)} %all-gather.9.cloned.1.call-done), kind=kOutput, calls=%fused_computation.73 | convolution fusion | flops 4305977344 | bytes 16777216 | tf_op jit(solution)/shard_map/dot_general | solution.py:30
  306.4 9.5 %fusion.8 = bf16[512,4096]{1,0:T(8,128)(2,1)} fusion(bf16[512,1024]{1,0:T(8,128)(2,1)S(1)} %get-tuple-element.13, bf16[1,4096,1024]{2,1,0:T(8,128)(2,1)} %all-gather.9.cloned.1.call-done), kind=kOutput, calls=%fused_computation.10 | convolution fusion | flops 4297064448 | bytes 13631488 | tf_op jit(solution)/shard_map/dot_general | solution.py:44
  315.9 0.0 reduce-scatter.6.cloned.1.call-start
  316.0 42.7 %reduce-scatter.4.cloned.1.call-done = bf16[128,4096]{1,0:T(8,128)(2,1)} async-done(((bf16[512,4096]{1,0:T(8,128)(2,1)}), bf16[128,4096]{1,0:T(8,128)(2,1)}) %reduce-scatter.4.cloned.1.call-update) | async-done | bytes 1048592 | tf_op jit(solution)/shard_map/reduce_scatter | solution.py:43
  358.7 1.7 fusion.44
  360.4 0.7 fusion.20
  361.2 5.5 collective-permute-start.1
  367.3 21.2 %collective-permute-done.1 = bf16[128,4096]{1,0:T(8,128)(2,1)S(1)} collective-permute-done((bf16[128,4096]{1,0:T(8,128)(2,1)S(1)}, bf16[128,4096]{1,0:T(8,128)(2,1)S(1)}, u32[]{:S(2)}, u32[]{:S(2)}) %collective-permute-start.1) | collective-permute-done | bytes 1048608 | tf_op jit(solution)/shard_map/ppermute | solution.py:14
  388.5 0.3 fusion.57
  388.9 0.1 copy.18
  389.0 16.1 %all_to_all.54 = bf16[128,4,1024]{2,0,1:T(8,128)(2,1)S(1)} all-to-all(bf16[128,4,1024]{2,0,1:T(8,128)(2,1)S(1)} %bitcast.101), channel_id=1, replica_groups=mesh['dp'=4,'section'=16,'tensor'=4] {'tensor'}, dimensions={1} | all-to-all | bytes 2097152 | tf_op jit(solution)/shard_map/all_to_all | solution.py:39
  405.0 1.6 fusion.48
  406.7 1.0 copy-done.5
  407.6 9.5 %fusion.11 = bf16[512,4096]{1,0:T(8,128)(2,1)} fusion(bf16[512,1024]{1,0:T(8,128)(2,1)S(1)} %get-tuple-element.7, bf16[1,4096,1024]{2,1,0:T(8,128)(2,1)} %all-gather.9.cloned.1.call-done), kind=kOutput, calls=%fused_computation.11 | convolution fusion | flops 4297064448 | bytes 13631488 | tf_op jit(solution)/shard_map/dot_general | solution.py:44
  417.2 0.0 reduce-scatter.8.cloned.1.call-start
  417.2 10.3 %multiply_convert_fusion = bf16[4096,1024]{1,0:T(8,128)(2,1)} fusion(bf16[512,4096]{1,0:T(8,128)(2,1)} %all-gather.7.cloned.1.call-done, bf16[512,1024]{1,0:T(8,128)(2,1)} %copy-done.5), kind=kOutput, calls=%fused_computation | convolution fusion | flops 4303355904 | bytes 13631488 | tf_op jit(solution)/shard_map/dot_general | solution.py:84
  427.5 27.9 %all_to_all.55 = bf16[4,128,1024]{2,1,0:T(8,128)(2,1)S(1)} all-to-all(bf16[4,128,1024]{2,1,0:T(8,128)(2,1)S(1)} %bitcast.100), channel_id=1, replica_groups=mesh['dp'=4,'section'=16,'tensor'=4] {'tensor'}, dimensions={0} | all-to-all | bytes 2097152 | tf_op jit(solution)/shard_map/all_to_all | solution.py:32
  455.4 0.2 convert_bitcast_fusion
  455.7 1.5 copy.16
  457.1 20.4 %reduce-scatter.6.cloned.1.call-done = bf16[128,4096]{1,0:T(8,128)(2,1)} async-done(((bf16[512,4096]{1,0:T(8,128)(2,1)}), bf16[128,4096]{1,0:T(8,128)(2,1)}) %reduce-scatter.6.cloned.1.call-update) | async-done | bytes 1048592 | tf_op jit(solution)/shard_map/reduce_scatter | solution.py:43
  477.5 3.4 fusion.45
  480.9 1.8 fusion.62
  482.7 129.1 %reduce-scatter.8.cloned.1.call-done = bf16[1024,1024]{1,0:T(8,128)(2,1)} async-done(((bf16[4096,1024]{1,0:T(8,128)(2,1)}), bf16[1024,1024]{1,0:T(8,128)(2,1)}) %reduce-scatter.8.cloned.1.call-update) | async-done | bytes 2097168 | tf_op jit(solution)/shard_map/reduce_scatter | solution.py:82
  611.8 7.0 %fusion.56 = bf16[1,1024,1024]{2,1,0:T(8,128)(2,1)} fusion(bf16[1,1024,1024]{2,1,0:T(8,128)(2,1)} %param.11, bf16[1024,1024]{1,0:T(8,128)(2,1)} %reduce-scatter.8.cloned.1.call-done, bf16[1,1024,1024]{2,1,0:T(8,128)(2,1)} %param.10), kind=kLoop, calls=%fused_computation.82 | loop fusion | flops 13631488 | bytes 8388608 | tf_op jit(solution)/shard_map/broadcast_in_dim | solution.py:99
  (22 shorter events, 0.2 us)
Async XLA Ops:
  7.2 59.6 %all-gather.5.cloned.1.call-start = ((), (), s32[]{:S(2)}) async-start(), calls=%async_computation.7 | async-start | bytes 5242880 | tf_op jit(solution)/shard_map/all_gather | solution.py:29
  12.0 170.9 %all-gather.9.cloned.1.call-start = ((), (), s32[]{:S(2)}) async-start(), calls=%async_computation.12 | async-start | bytes 10485760 | tf_op jit(solution)/shard_map/all_gather | solution.py:69
  12.8 282.0 %all-gather.7.cloned.1.call-start = ((), (), s32[]{:S(2)}) async-start(), calls=%async_computation.8 | async-start | bytes 5242880 | tf_op jit(solution)/shard_map/all_gather | solution.py:29
  211.2 1.2 copy-start
  212.4 0.7 copy-start.6
  212.7 27.2 %collective-permute-start = (bf16[128,4096]{1,0:T(8,128)(2,1)S(1)}, bf16[128,4096]{1,0:T(8,128)(2,1)S(1)}, u32[]{:S(2)}, u32[]{:S(2)}) collective-permute-start(bf16[128,4096]{1,0:T(8,128)(2,1)S(1)} %fusion.29), channel_id=1, source_target_pairs={{0,4},{4,8},{8,12},{12,16},{16,20},{20,24},{24,28},{28,32},{32,36}... | collective-permute-start | bytes 3145736 | tf_op jit(solution)/shard_map/ppermute | solution.py:14
  240.4 1.4 copy-start.1
  241.7 116.9 %reduce-scatter.4.cloned.1.call-start = ((), (), s32[]{:S(2)}) async-start(), calls=%async_computation.9 | async-start | bytes 5242880 | tf_op jit(solution)/shard_map/reduce_scatter | solution.py:43
  315.9 161.6 %reduce-scatter.6.cloned.1.call-start = ((), (), s32[]{:S(2)}) async-start(), calls=%async_computation.10 | async-start | bytes 5242880 | tf_op jit(solution)/shard_map/reduce_scatter | solution.py:43
  358.7 1.7 copy-start.2
  361.2 27.4 %collective-permute-start.1 = (bf16[128,4096]{1,0:T(8,128)(2,1)S(1)}, bf16[128,4096]{1,0:T(8,128)(2,1)S(1)}, u32[]{:S(2)}, u32[]{:S(2)}) collective-permute-start(bf16[128,4096]{1,0:T(8,128)(2,1)S(1)} %fusion.20), channel_id=1, source_target_pairs={{0,60},{4,0},{8,4},{12,8},{16,12},{20,16},{24,20},{28,24},{32,28},... | collective-permute-start | bytes 3145736 | tf_op jit(solution)/shard_map/ppermute | solution.py:14
  388.9 16.2 %copy-start.4 = (f32[512,1024]{1,0:T(8,128)S(1)}, f32[512,1024]{1,0:T(8,128)}, u32[]{:S(2)}) copy-start(f32[512,1024]{1,0:T(8,128)} %get-tuple-element.14) | copy-start | bytes 6291460
  406.7 1.0 copy-start.5
  417.2 194.6 %reduce-scatter.8.cloned.1.call-start = ((), (), s32[]{:S(2)}) async-start(), calls=%async_computation.11 | async-start | bytes 10485760 | tf_op jit(solution)/shard_map/reduce_scatter | solution.py:82
  477.5 3.4 copy-start.3
Sparse Core Ops, SparseCore 0:
  12.2 54.5 all-gather.4
  68.6 114.3 all-gather.8
  241.9 52.8 all-gather.6
  316.1 42.5 reduce-scatter.3
  417.3 60.1 reduce-scatter.5
  480.2 131.6 reduce-scatter.7

commit v2 on v1

v2 whole, which is shorter than its diff:
```python
import functools

import jax
import jax.numpy as jnp
from jax import lax
from jax.experimental import pallas as pl
from jax.experimental.pallas import tpu as pltpu
from jax.sharding import PartitionSpec as P

EPSILON = 1e-05
BETA_ONE = 0.9
BETA_TWO = 0.95
GELU_SCALE = 0.7978845608028654
GELU_CUBE = 0.044715

D = 4096
CH = 4
ROWS = 128
SLAB = 32
COLS = 1024
TILE = 256
MESH = pl.DeviceIdType.MESH

(W_ANTI, W_FWD, W_SIB, X_ROWS, C_COLS, PRIOR_MOVE, GATHER_R, GATHER_L, RELAY_R, RELAY_L, Y_ONE, Y_TWO, Y_THREE,
 OPP_R, OPP_L, SUM_R, SUM_L, CARRY_MOVE, ROW_OPP_R, ROW_OPP_L, ROW_SUM_R, ROW_SUM_L, HG_SIB, HG_ANTI, HG_FWD,
 N_ANTI, N_SIB, N_R, N_L, N_RELAY_R, N_RELAY_L, N_SHARE) = range(32)


def gelu(v):
    return 0.5 * v * (1.0 + jnp.tanh(GELU_SCALE * (v + GELU_CUBE * v * v * v)))


def gelu_slope(v):
    square = v * v
    th = jnp.tanh(GELU_SCALE * v * (1.0 + GELU_CUBE * square))
    return 0.5 * (1.0 + th) + (0.5 * GELU_SCALE) * v * (1.0 - th * th) * (1.0 + 3.0 * GELU_CUBE * square)


def f32(v):
    return v.astype(jnp.float32)


def bf16(v):
    return v.astype(jnp.bfloat16)


def kernel(
    x_ref, cot_ref, w_ref, m1_ref, m2_ref, gain_ref, flag_ref,
    y_ref, dx_ref, upd_ref,
    w_all, x_all, in_all, nrm, hid, cot, prior, incoming, first_out, y_cols, carry,
    opp, to_r, to_l, own, got_a, got_b, got_l, got_r,
    part, row_a, row_b, row_l, row_r,
    hg, hg_sib, hg_anti, hg_other, hg_early, n_sib, n_anti, n_other, inv_s, dx_buf, m1_buf, m2_buf, upd_buf,
    send_sem, recv_sem, local_sem,
):
    t = lax.axis_index("tensor")
    d = lax.axis_index("dp")
    s = lax.axis_index("section")
    right, left, across = lax.rem(t + 1, 4), lax.rem(t + 3, 4), lax.rem(t + 2, 4)
    core = lax.rem(d, 2)
    half = d // 2
    sib = d + 1 - 2 * core
    anti = lax.rem(d + 2, 4)
    anti_sib = lax.rem(sib + 2, 4)
    after = lax.rem(s + 1, 16)
    before = lax.rem(s + 15, 16)
    to_right, to_left = {"tensor": right}, {"tensor": left}
    to_sib, to_anti = {"dp": sib}, {"dp": anti}
    to_after, to_before = {"section": after}, {"section": before}

    def cols(block):
        return pl.ds(pl.multiple_of(block * COLS, COLS), COLS)

    def tile(block, n):
        return pl.ds(pl.multiple_of(block * COLS + n * TILE, TILE), TILE)

    def copy(kind, index, src, dst, device):
        return pltpu.make_async_remote_copy(
            src_ref=src, dst_ref=dst, send_sem=send_sem.at[kind, index], recv_sem=recv_sem.at[kind, index],
            device_id=device, device_id_type=MESH,
        )

    def arrived(kind, index, where):
        copy(kind, index, where, where, to_sib).wait_recv()

    def sent(kind, index, where):
        copy(kind, index, where, where, to_sib).wait_send()

    barrier = pltpu.get_barrier_semaphore()
    for device in (to_right, to_left, {"tensor": across}, to_sib, to_anti, to_after, to_before):
        pl.semaphore_signal(barrier, inc=1, device_id=device, device_id_type=MESH)
    pl.semaphore_wait(barrier, 7)

    def rows_of(block, k):
        return pl.ds(pl.multiple_of(block * COLS + k * TILE, TILE), TILE)

    for k in range(4):
        copy(W_ANTI, k, w_ref.at[pl.ds(k * TILE, TILE)], w_all.at[rows_of(d, k)], to_anti).start()
    copy(W_SIB, 0, w_ref, w_all.at[cols(d)], to_sib).start()
    for k in range(1, 4):
        copy(X_ROWS, k - 1, x_ref, x_all.at[:, t], {"tensor": lax.rem(t + k, 4)}).start()
    loads = [
        pltpu.make_async_copy(x_ref, x_all.at[:, t], local_sem.at[0]),
        pltpu.make_async_copy(w_ref, w_all.at[cols(d)], local_sem.at[1]),
        pltpu.make_async_copy(cot_ref.at[:, :, cols(t)], cot.at[:, t], local_sem.at[2]),
        pltpu.make_async_copy(m1_ref, m1_buf, local_sem.at[3]),
        pltpu.make_async_copy(m2_ref, m2_buf, local_sem.at[4]),
    ]
    for load in loads:
        load.start()
    for k in range(1, 4):
        peer = lax.rem(t + k, 4)
        copy(C_COLS, k - 1, cot_ref.at[:, :, cols(peer)], cot.at[:, t], {"tensor": peer}).start()

    def normalize(read, j):
        def squares(b, total):
            u = read(pl.ds(pl.multiple_of(b * 512, 512), 512))
            u = u * u
            return total + (u[:, 0:128] + u[:, 128:256]) + (u[:, 256:384] + u[:, 384:512])

        total = lax.fori_loop(0, 8, squares, jnp.zeros((ROWS, 128), jnp.float32))
        inv = lax.rsqrt(jnp.sum(total, axis=-1, keepdims=True) * (1.0 / D) + EPSILON)

        def scale(b, _):
            where = pl.ds(pl.multiple_of(b * 512, 512), 512)
            nrm[j, :, :, where] = bf16(read(where) * inv * gain_ref[:, where]).reshape(4, SLAB, 512)
            return 0

        lax.fori_loop(0, 8, scale, 0)
        return inv

    loads[0].wait()
    for k in range(1, 4):
        arrived(X_ROWS, k - 1, x_all.at[:, lax.rem(t + 4 - k, 4)])

    def first_norm(j, _):
        normalize(lambda where: f32(x_all[j, :, :, where]).reshape(ROWS, -1), j)
        return 0

    lax.fori_loop(0, CH, first_norm, 0)

    def add_rows(block, k, clear=False):
        rows = rows_of(block, k)

        def step(n, _):
            there = pl.ds(pl.multiple_of(n * TILE, TILE), TILE)
            product = jnp.dot(
                nrm[:, :, :, rows].reshape(CH * ROWS, TILE), w_all[rows, there], preferred_element_type=jnp.float32
            ).reshape(CH, ROWS, TILE)
            if clear:
                hid[:, :, there] = product
            else:
                hid[:, :, there] += product
            return 0

        lax.fori_loop(0, 4, step, 0)

    loads[1].wait()
    add_rows(d, 0, clear=True)
    lax.fori_loop(1, 4, lambda k, _: (add_rows(d, k), 0)[1], 0)
    arrived(W_SIB, 0, w_all.at[cols(sib)])
    lax.fori_loop(0, 4, lambda k, _: (add_rows(sib, k), 0)[1], 0)
    loads[2].wait()
    for k in range(1, 4):
        arrived(C_COLS, k - 1, cot.at[:, lax.rem(t + 4 - k, 4)])

    def take(k, _):
        theirs = w_all.at[rows_of(anti, k)]
        arrived(W_ANTI, k, theirs)
        copy(W_FWD, k, theirs, theirs, to_sib).start()
        add_rows(anti, k)
        arrived(W_FWD, k, w_all.at[rows_of(anti_sib, k)])
        add_rows(anti_sib, k)
        return 0

    lax.fori_loop(0, 4, take, 0)

    def first_step(j, _):
        def step(n, _):
            there = pl.ds(pl.multiple_of(n * TILE, TILE), TILE)
            branch = f32(bf16(gelu(hid[j, :, there])))
            first_out[j, :, there] = bf16(f32(x_all[j, :, :, tile(t, n)]).reshape(ROWS, TILE) + branch)
            return 0

        lax.fori_loop(0, 4, step, 0)
        copy(PRIOR_MOVE, j, first_out.at[j], prior.at[j], to_after).start()
        return 0

    lax.fori_loop(0, CH, first_step, 0)

    def choose(j):
        arrived(PRIOR_MOVE, j, prior.at[j])

        def step(n, _):
            there = pl.ds(pl.multiple_of(n * TILE, TILE), TILE)
            mask = jnp.broadcast_to(flag_ref[0:1, 0:TILE], (ROWS, TILE)) > 0.5
            plain = f32(x_all[j, :, :, tile(t, n)]).reshape(ROWS, TILE)
            in_all[j, :, tile(t, n)] = bf16(jnp.where(mask, f32(prior[j, :, there]), plain))
            return 0

        lax.fori_loop(0, 4, step, 0)
        mine = in_all.at[j, :, cols(t)]
        copy(GATHER_R, j, mine, mine, to_right).start()
        copy(GATHER_L, j, mine, mine, to_left).start()

    def relay(j):
        arrived(GATHER_R, j, in_all.at[j, :, cols(left)])
        low = in_all.at[j, pl.ds(0, 64), cols(left)]
        copy(RELAY_R, j, low, low, to_right).start()
        arrived(GATHER_L, j, in_all.at[j, :, cols(right)])
        high = in_all.at[j, pl.ds(64, 64), cols(right)]
        copy(RELAY_L, j, high, high, to_left).start()

    def input_grad_tile(source, block, m, j, inv, slope):
        rows = tile(block, m)
        normed_grad = lax.dot_general(
            source, w_all[rows, :], (((1,), (1,)), ((), ())), preferred_element_type=jnp.float32
        )
        return normed_grad * (inv * gain_ref[:, rows]) - f32(in_all[j, :, rows]) * slope

    def forward(j):
        arrived(RELAY_R, j, in_all.at[j, pl.ds(0, 64), cols(across)])
        arrived(RELAY_L, j, in_all.at[j, pl.ds(64, 64), cols(across)])
        inv = normalize(lambda where: f32(in_all[j, :, where]), j)
        inv_s[j] = inv
        crossing = pl.ds(pl.multiple_of((1 - half) * 2048, 2048), 2048)
        copy(N_ANTI, j, nrm.at[j, t, :, crossing], n_anti.at[j, t], to_anti).start()
        copy(N_SIB, j, nrm.at[j, :, :, cols(sib)], n_sib.at[j], to_sib).start()

        def step(n, total):
            there = pl.ds(pl.multiple_of(n * TILE, TILE), TILE)
            hidden = jnp.dot(nrm[j].reshape(ROWS, D), w_all[:, there], preferred_element_type=jnp.float32)
            hid[j, :, there] = hidden
            branch = f32(bf16(gelu(hidden)))
            y_cols[j, :, :, there] = bf16(f32(in_all[j, :, tile(t, n)]) + branch).reshape(4, SLAB, TILE)
            upstream = f32(cot[j, :, :, there]).reshape(ROWS, TILE)
            grad = bf16(upstream * gelu_slope(hidden))
            hg_early[:, there] = grad
            return total + jnp.sum(f32(grad) * hidden, axis=-1, keepdims=True)

        total = lax.fori_loop(0, 4, step, jnp.zeros((ROWS, 1), jnp.float32))
        slope = inv * inv * total * (1.0 / D)

        def fill(target, block):
            def step(m, _):
                there = pl.ds(pl.multiple_of(m * TILE, TILE), TILE)
                target[j, :, there] = bf16(input_grad_tile(hg_early[...], block, m, j, inv, slope))
                return 0

            lax.fori_loop(0, 4, step, 0)

        fill(opp, across)
        copy(OPP_R, j, opp.at[j, pl.ds(0, 64)], got_a.at[j], to_right).start()
        copy(OPP_L, j, opp.at[j, pl.ds(64, 64)], got_b.at[j], to_left).start()
        fill(to_r, right)
        fill(to_l, left)
        fill(own, t)
        for k in range(1, 4):
            peer = lax.rem(t + k, 4)
            copy(Y_ONE + k - 1, j, y_cols.at[j, peer], y_ref.at[j, :, cols(t)], {"tensor": peer}).start()
        pltpu.make_async_copy(y_cols.at[j, t], y_ref.at[j, :, cols(t)], local_sem.at[5 + j]).start()

    def add_halves(j):
        arrived(OPP_R, j, got_a.at[j])
        to_r[j, 0:64, :] = bf16(f32(to_r[j, 0:64, :]) + f32(got_a[j]))
        copy(SUM_R, j, to_r.at[j], got_l.at[j], to_right).start()
        arrived(OPP_L, j, got_b.at[j])
        to_l[j, 64:128, :] = bf16(f32(to_l[j, 64:128, :]) + f32(got_b[j]))
        copy(SUM_L, j, to_l.at[j], got_r.at[j], to_left).start()

    def carry_on(j):
        arrived(SUM_R, j, got_l.at[j])
        arrived(SUM_L, j, got_r.at[j])

        def step(n, _):
            there = pl.ds(pl.multiple_of(n * TILE, TILE), TILE)
            total = (f32(got_l[j, :, there]) + f32(got_r[j, :, there])) + f32(own[j, :, there])
            carry[j, :, there] = bf16(f32(cot[j, :, :, there]).reshape(ROWS, TILE) + total)
            return 0

        lax.fori_loop(0, 4, step, 0)
        copy(CARRY_MOVE, j, carry.at[j], incoming.at[j], to_before).start()

    def backward(j):
        arrived(CARRY_MOVE, j, incoming.at[j])

        def step(n, total):
            there = pl.ds(pl.multiple_of(n * TILE, TILE), TILE)
            mask = jnp.broadcast_to(flag_ref[1:2, 0:TILE], (ROWS, TILE)) > 0.5
            upstream = f32(cot[j, :, :, there]).reshape(ROWS, TILE)
            summed = bf16(upstream + jnp.where(mask, f32(incoming[j, :, there]), 0.0))
            incoming[j, :, there] = summed
            hidden = hid[j, :, there]
            grad = bf16(f32(summed) * gelu_slope(hidden))
            hg[j, :, there] = grad
            return total + jnp.sum(f32(grad) * hidden, axis=-1, keepdims=True)

        total = lax.fori_loop(0, 4, step, jnp.zeros((ROWS, 1), jnp.float32))
        copy(HG_ANTI, j, hg.at[j], hg_anti.at[j], to_anti).start()
        copy(HG_SIB, j, hg.at[j], hg_sib.at[j], to_sib).start()
        inv = inv_s[j]
        slope = inv * inv * total * (1.0 / D)

        def other(q, _):
            block = lax.rem(t + 1 + q // 4, 4)
            m = lax.rem(q, 4)
            value = bf16(input_grad_tile(hg[j], block, m, j, inv, slope))
            part[j, :, :, tile(block, m)] = value.reshape(4, SLAB, TILE)
            return 0

        lax.fori_loop(0, 12, other, 0)

        def mine(m, _):
            there = pl.ds(pl.multiple_of(m * TILE, TILE), TILE)
            value = input_grad_tile(hg[j], t, m, j, inv, slope) + f32(incoming[j, :, there])
            part[j, :, :, tile(t, m)] = bf16(value).reshape(4, SLAB, TILE)
            return 0

        lax.fori_loop(0, 4, mine, 0)
        copy(ROW_OPP_R, j, part.at[j, across, pl.ds(0, 16)], row_a.at[j], to_right).start()
        copy(ROW_OPP_L, j, part.at[j, across, pl.ds(16, 16)], row_b.at[j], to_left).start()

    def add_row_halves(j):
        arrived(ROW_OPP_R, j, row_a.at[j])
        part[j, right, 0:16, :] = bf16(f32(part[j, right, 0:16, :]) + f32(row_a[j]))
        copy(ROW_SUM_R, j, part.at[j, right], row_l.at[j], to_right).start()
        arrived(ROW_OPP_L, j, row_b.at[j])
        part[j, left, 16:32, :] = bf16(f32(part[j, left, 16:32, :]) + f32(row_b[j]))
        copy(ROW_SUM_L, j, part.at[j, left], row_r.at[j], to_left).start()

    def finish_rows(j):
        arrived(ROW_SUM_R, j, row_l.at[j])
        arrived(ROW_SUM_L, j, row_r.at[j])

        def step(b, _):
            there = pl.ds(pl.multiple_of(b * 1024, 1024), 1024)
            total = (f32(row_l[j, :, there]) + f32(row_r[j, :, there])) + f32(part[j, t, :, there])
            mask = jnp.broadcast_to(flag_ref[0:1, 0:1024], (SLAB, 1024)) > 0.5
            dx_buf[j, :, there] = bf16(jnp.where(mask, 0.0, total))
            return 0

        lax.fori_loop(0, 4, step, 0)
        pltpu.make_async_copy(dx_buf.at[j], dx_ref.at[j], local_sem.at[9 + j]).start()

    def spread_normed(j):
        arrived(N_ANTI, j, n_anti.at[j, t])
        copy(N_R, j, n_anti.at[j, t], n_anti.at[j, t], to_right).start()
        copy(N_L, j, n_anti.at[j, t], n_anti.at[j, t], to_left).start()

    def relay_normed(j):
        arrived(N_R, j, n_anti.at[j, left])
        low = n_anti.at[j, left, pl.ds(0, 16)]
        copy(N_RELAY_R, j, low, low, to_right).start()
        arrived(N_L, j, n_anti.at[j, right])
        high = n_anti.at[j, right, pl.ds(16, 16)]
        copy(N_RELAY_L, j, high, high, to_left).start()

    def share_normed(j):
        arrived(N_RELAY_R, j, n_anti.at[j, across, pl.ds(0, 16)])
        arrived(N_RELAY_L, j, n_anti.at[j, across, pl.ds(16, 16)])
        theirs = pl.ds(pl.multiple_of((1 - core) * COLS, COLS), COLS)
        copy(N_SHARE, j, n_anti.at[j, :, :, theirs], n_other.at[j], to_sib).start()

    def pass_grad(j):
        arrived(HG_ANTI, j, hg_anti.at[j])
        copy(HG_FWD, j, hg_anti.at[j], hg_other.at[j], to_sib).start()

    def stage(run, j):
        pl.when(jnp.logical_and(j >= 0, j < CH))(lambda: run(j))

    def turn(i, _):
        stage(choose, i)
        stage(add_halves, i - 1)
        stage(backward, i - 2)
        stage(relay, i)
        stage(spread_normed, i - 1)
        stage(add_row_halves, i - 2)
        stage(carry_on, i - 1)
        stage(relay_normed, i - 2)
        stage(finish_rows, i - 3)
        stage(pass_grad, i - 3)
        stage(share_normed, i - 3)
        stage(forward, i)
        return 0

    lax.fori_loop(0, CH + 3, turn, 0)

    def last_arrivals(j, _):
        arrived(HG_SIB, j, hg_sib.at[j])
        arrived(HG_FWD, j, hg_other.at[j])
        arrived(N_SIB, j, n_sib.at[j])
        arrived(N_SHARE, j, n_other.at[j])
        return 0

    lax.fori_loop(0, CH, last_arrivals, 0)
    loads[3].wait()
    loads[4].wait()

    def product(left_rows, right_rows):
        return lax.dot_general(
            left_rows.reshape(CH * ROWS, TILE), right_rows.reshape(CH * ROWS, 512),
            (((0,), (0,)), ((), ())), preferred_element_type=jnp.float32,
        )

    def step_dir(q, _):
        f = q // 2
        rows = pl.ds(pl.multiple_of(f * TILE, TILE), TILE)
        there = pl.ds(pl.multiple_of(lax.rem(q, 2) * 512, 512), 512)
        total = product(nrm[:, :, :, tile(d, f)], hg[:, :, there])
        total += product(n_sib[:, :, :, rows], hg_sib[:, :, there])
        total += product(n_anti[:, :, :, tile(core, f)], hg_anti[:, :, there])
        total += product(n_other[:, :, :, rows], hg_other[:, :, there])
        total = total * (1.0 / (4 * CH * ROWS))
        first = BETA_ONE * f32(m1_buf[rows, there]) + (1.0 - BETA_ONE) * total
        second = BETA_TWO * f32(m2_buf[rows, there]) + (1.0 - BETA_TWO) * total * total
        upd_buf[rows, there] = bf16(first / (jnp.sqrt(second) + 1e-08))
        return 0

    lax.fori_loop(0, 8, step_dir, 0)
    out = pltpu.make_async_copy(upd_buf, upd_ref, local_sem.at[13])
    out.start()

    def drain(j, _):
        for k in range(1, 4):
            arrived(Y_ONE + k - 1, j, y_ref.at[j, :, cols(lax.rem(t + 4 - k, 4))])
            sent(Y_ONE + k - 1, j, y_cols.at[j, 0])
        pltpu.make_async_copy(y_cols.at[j, t], y_ref.at[j, :, cols(t)], local_sem.at[5 + j]).wait()
        pltpu.make_async_copy(dx_buf.at[j], dx_ref.at[j], local_sem.at[9 + j]).wait()
        sent(W_ANTI, j, w_all.at[rows_of(d, 0)])
        sent(W_FWD, j, w_all.at[rows_of(anti, j)])
        sent(PRIOR_MOVE, j, first_out.at[j])
        sent(GATHER_R, j, in_all.at[j, :, cols(t)])
        sent(GATHER_L, j, in_all.at[j, :, cols(t)])
        sent(RELAY_R, j, in_all.at[j, pl.ds(0, 64), cols(left)])
        sent(RELAY_L, j, in_all.at[j, pl.ds(64, 64), cols(right)])
        sent(OPP_R, j, opp.at[j, pl.ds(0, 64)])
        sent(OPP_L, j, opp.at[j, pl.ds(64, 64)])
        sent(SUM_R, j, to_r.at[j])
        sent(SUM_L, j, to_l.at[j])
        sent(CARRY_MOVE, j, carry.at[j])
        sent(ROW_OPP_R, j, part.at[j, across, pl.ds(0, 16)])
        sent(ROW_OPP_L, j, part.at[j, across, pl.ds(16, 16)])
        sent(ROW_SUM_R, j, part.at[j, right])
        sent(ROW_SUM_L, j, part.at[j, left])
        sent(HG_SIB, j, hg.at[j])
        sent(HG_ANTI, j, hg.at[j])
        sent(HG_FWD, j, hg_anti.at[j])
        sent(N_ANTI, j, n_anti.at[j, t])
        sent(N_SIB, j, n_sib.at[j])
        sent(N_R, j, n_anti.at[j, t])
        sent(N_L, j, n_anti.at[j, t])
        sent(N_RELAY_R, j, n_anti.at[j, left, pl.ds(0, 16)])
        sent(N_RELAY_L, j, n_anti.at[j, right, pl.ds(16, 16)])
        sent(N_SHARE, j, n_other.at[j])
        return 0

    lax.fori_loop(0, CH, drain, 0)
    sent(W_SIB, 0, w_all.at[cols(d)])
    for k in range(3):
        sent(X_ROWS, k, x_all.at[:, t])
        sent(C_COLS, k, cot.at[:, t])
    out.wait()


def whole(x, cot, w, m1, m2, gain, flags):
    def vm(*shape, dtype=jnp.bfloat16):
        return pltpu.VMEM(shape, dtype)

    scratch = [
        vm(D, COLS), vm(CH, 4, SLAB, D), vm(CH, ROWS, D), vm(CH, 4, SLAB, D),
        vm(CH, ROWS, COLS, dtype=jnp.float32), vm(CH, 4, SLAB, COLS),
        vm(CH, ROWS, COLS), vm(CH, ROWS, COLS), vm(CH, ROWS, COLS), vm(CH, 4, SLAB, COLS), vm(CH, ROWS, COLS),
        vm(CH, ROWS, COLS), vm(CH, ROWS, COLS), vm(CH, ROWS, COLS), vm(CH, ROWS, COLS),
        vm(CH, 64, COLS), vm(CH, 64, COLS), vm(CH, ROWS, COLS), vm(CH, ROWS, COLS),
        vm(CH, 4, SLAB, D), vm(CH, 16, D), vm(CH, 16, D), vm(CH, SLAB, D), vm(CH, SLAB, D),
        vm(CH, ROWS, COLS), vm(CH, ROWS, COLS), vm(CH, ROWS, COLS), vm(CH, ROWS, COLS), vm(ROWS, COLS),
        vm(CH, 4, SLAB, COLS), vm(CH, 4, SLAB, 2 * COLS), vm(CH, 4, SLAB, COLS),
        vm(CH, ROWS, 1, dtype=jnp.float32), vm(CH, SLAB, D), vm(COLS, COLS), vm(COLS, COLS), vm(COLS, COLS),
        pltpu.SemaphoreType.DMA((32, CH)), pltpu.SemaphoreType.DMA((32, CH)), pltpu.SemaphoreType.DMA((14,)),
    ]
    anywhere = pl.BlockSpec(memory_space=pl.ANY)
    near = pl.BlockSpec(memory_space=pltpu.VMEM)
    return pl.pallas_call(
        kernel,
        out_shape=(
            jax.ShapeDtypeStruct((CH, SLAB, D), jnp.bfloat16),
            jax.ShapeDtypeStruct((CH, SLAB, D), jnp.bfloat16),
            jax.ShapeDtypeStruct((COLS, COLS), jnp.bfloat16),
        ),
        in_specs=[anywhere] * 5 + [near] * 2,
        out_specs=(anywhere,) * 3,
        scratch_shapes=scratch,
        compiler_params=pltpu.CompilerParams(
            collective_id=0, has_side_effects=True, vmem_limit_bytes=63 * 2**20
        ),
        cost_estimate=pl.CostEstimate(flops=21 * 10**9, bytes_accessed=20 * 2**20, transcendentals=2 * 10**6),
    )(x, cot, w, m1, m2, gain, flags)


def body(x_in, gain, weight, moment_one, moment_two, cotangent, preempted):
    section_here = lax.axis_index("section")
    flag_row = lax.dynamic_index_in_dim(preempted, lax.axis_index("dp"), 0, keepdims=False)
    flag_self = lax.dynamic_index_in_dim(flag_row, section_here, 0, keepdims=False)
    flag_next = lax.dynamic_index_in_dim(flag_row, (section_here + 1) % 16, 0, keepdims=False)
    flags = jnp.stack([flag_self, flag_next]).astype(jnp.float32)
    flags = jnp.broadcast_to(flags[:, None], (2, COLS))
    y, dx, update = whole(
        x_in.reshape(CH, SLAB, D), cotangent.reshape(CH, SLAB, D), weight[0], moment_one[0], moment_two[0],
        gain.astype(jnp.float32), flags,
    )
    return (y.reshape(1, CH * SLAB, D), dx.reshape(1, CH * SLAB, D), update[None])


def solution(mesh):
    placed = (
        P("section", ("dp", "tensor"), None),
        P("section", None),
        P("section", "dp", "tensor"),
        P("section", "dp", "tensor"),
        P("section", "dp", "tensor"),
        P("section", ("dp", "tensor"), None),
        P(),
    )
    return jax.shard_map(
        body,
        mesh=mesh,
        in_specs=placed,
        out_specs=(
            P("section", ("dp", "tensor"), None),
            P("section", ("dp", "tensor"), None),
            P("section", "dp", "tensor"),
        ),
        check_vma=False,
    )
```

time: 626 us -> 298 us (0.48)
  waiting for transfers between devices: 442 us -> 0 us
  Pallas kernels: 0 us -> 286 us
  blocking collectives: 81.8 us -> 0 us
  matrix products: 50.5 us -> 0 us
  other arithmetic: 23.8 us -> 2.7 us
  between operations: 15.6 us -> 0.68 us
    pallas_call x0 -> x1, Pallas kernels: none -> 286 us  [whole(): pl.pallas_call(kernel, out_shape=(jax.ShapeDtypeStruct((CH, SLAB, D), jnp...]
    all_gather x3 -> x0, waiting for transfers between devices: 203 us -> none  [the longest x1 116 us: body(): weight_cols = lax.all_gather(weight_shard, 'dp', axis=0, tiled=True)]
    reduce_scatter x3 -> x0, waiting for transfers between devices: 192 us -> none  [the longest x1 129 us: body(): lax.psum_scatter((lax.dot_general(normed_all, hidden_grad, (((0,), (0,)),...]
    all_to_all x4 -> x0, blocking collectives: 81.8 us -> none  [the longest x2 46.3 us: forward_part(): lax.all_to_all(branch, 'tensor', split_axis=0, concat_axis=1, tiled=True)]
    dot_general x5 -> x0, matrix products: 50.5 us -> none  [the longest x2 21.2 us: forward_part(): jnp.dot(normed_all, weight_cols, preferred_element_type=jnp.float32)]
    ppermute x2 -> x0, waiting for transfers between devices: 46.8 us -> none  [from_behind(): return lax.ppermute(value, axis, pairs)]
    broadcast_in_dim x2 -> x0, other arithmetic: 8.72 us -> none  [body(): return (section_out[None], grad_in[None], step_dir[None])]
    reduce_sum x4 -> x0, other arithmetic: 7.12 us -> none  [the longest x2 5.14 us: normalize(): return widened * inverse * gain_row.astype(jnp.float32)]
  transfers between devices with their start and end apart: 8 -> 0, of which waited for: 8 -> 0; matrix products, arithmetic and copies ran while one was open for 3% -> 0% of each run, Pallas kernels for 0% -> 0%
where the time goes in v2:
time: 298 us; the launch traced here: 296 us
  Pallas kernels  286 us (96%)
  local copies, waits for them, and re-layouts  6.76 us (2%)
    pallas_call x1, Pallas kernels, whole(): pl.pallas_call(kernel, out_shape=(jax.ShapeDtypeStruct((CH, SLAB, D), jnp...  286 us

profile of v2, /device:TPU:1, one launch (start us, length us, event | category | flops | bytes accessed | tf_op | source)
XLA Modules:
  0.0 296.0 jit_solution(4937803155373931951)
XLA Ops:
  0.7 1.4 fusion
  2.0 1.4 add_convert_fusion
  3.4 0.7 broadcast_in_dim.4.flag_ref
  4.0 1.3 convert_element_type.10.gain_ref
  5.4 285.9 %shard_map.94 = (bf16[4,32,4096]{2,1,0:T(8,128)(2,1)}, bf16[4,32,4096]{2,1,0:T(8,128)(2,1)}, bf16[1024,1024]{1,0:T(8,128)(2,1)}) custom-call(bf16[4,32,4096]{2,1,0:T(8,128)(2,1)} %bitcast.16, bf16[4,32,4096]{2,1,0:T(8,128)(2,1)} %bitcast.17, bf16[1024,1024]{1,0:T(8,128)(2,1)} %bitcast.13, bf16[1024,1024]{1,0:T(8,128)(2,1)} %bitcast.14, ...), custom_call_target="tpu_custom_call" | custom-call | flops 20999999488 | bytes 20971520 | tf_op jit(solution)/shard_map/pallas_call | solution.py:483
  291.3 0.0 copy-start.1
  291.3 0.0 copy-start
  291.3 2.4 copy.13
  293.7 0.0 copy-done.1
  293.7 1.0 copy.14
  294.7 0.0 copy-done
  294.7 1.3 copy.15
Async XLA Ops:
  291.3 2.5 copy-start.1
  291.3 3.4 %copy-start = (bf16[1024,1024]{1,0:T(8,128)(2,1)S(1)}, bf16[1024,1024]{1,0:T(8,128)(2,1)}, u32[]{:S(2)}) copy-start(bf16[1024,1024]{1,0:T(8,128)(2,1)} %get-tuple-element.8) | copy-start | bytes 6291460

commit v3 on v2

v3 whole, which is shorter than its diff:
```python
import jax
import jax.numpy as jnp
from jax import lax
from jax.experimental import pallas as pl
from jax.experimental.pallas import tpu as pltpu
from jax.sharding import PartitionSpec as P

EPSILON = 1e-05
BETA_ONE = 0.9
BETA_TWO = 0.95
GELU_SCALE = 0.7978845608028654
GELU_CUBE = 0.044715

D = 4096
CH = 4
ROWS = 128
SLAB = 32
COLS = 1024
TILE = 256
MESH = pl.DeviceIdType.MESH

(W_ANTI, W_FWD, W_SIB, X_ONE, X_TWO, X_THREE, C_COLS, PRIOR_MOVE, GATHER_R, GATHER_L, RELAY_R, RELAY_L,
 Y_ONE, Y_TWO, Y_THREE,
 OPP_R, OPP_L, SUM_R, SUM_L, CARRY_MOVE, ROW_OPP_R, ROW_OPP_L, ROW_SUM_R, ROW_SUM_L, HG_SIB, HG_ANTI, HG_FWD,
 N_ANTI, N_SIB, N_R, N_L, N_RELAY_R, N_RELAY_L, N_SHARE) = range(34)


def gelu(v):
    return 0.5 * v * (1.0 + jnp.tanh(GELU_SCALE * (v + GELU_CUBE * v * v * v)))


def gelu_slope(v):
    square = v * v
    th = jnp.tanh(GELU_SCALE * v * (1.0 + GELU_CUBE * square))
    return 0.5 * (1.0 + th) + (0.5 * GELU_SCALE) * v * (1.0 - th * th) * (1.0 + 3.0 * GELU_CUBE * square)


def f32(v):
    return v.astype(jnp.float32)


def bf16(v):
    return v.astype(jnp.bfloat16)


def kernel(
    x_ref, cot_ref, w_ref, m1_ref, m2_ref, gain_ref, flag_ref,
    y_ref, dx_ref, upd_ref,
    w_all, w_t, x_all, in_all, nrm, hid, cot, prior, incoming, y_cols,
    opp, to_r, to_l, own, got_a, got_b, got_l, got_r,
    part, row_a, row_b, row_l, row_r,
    hg, hg_sib, hg_anti, hg_other, n_sib, n_anti, n_other, inv_s, total_s,
    send_sem, recv_sem, local_sem,
):
    t = lax.axis_index("tensor")
    d = lax.axis_index("dp")
    s = lax.axis_index("section")
    right, left, across = lax.rem(t + 1, 4), lax.rem(t + 3, 4), lax.rem(t + 2, 4)
    core = lax.rem(d, 2)
    half = d // 2
    sib = d + 1 - 2 * core
    anti = lax.rem(d + 2, 4)
    anti_sib = lax.rem(sib + 2, 4)
    after = lax.rem(s + 1, 16)
    before = lax.rem(s + 15, 16)
    to_right, to_left = {"tensor": right}, {"tensor": left}
    to_sib, to_anti = {"dp": sib}, {"dp": anti}
    to_after, to_before = {"section": after}, {"section": before}

    def cols(block):
        return pl.ds(pl.multiple_of(block * COLS, COLS), COLS)

    def tile(block, n):
        return pl.ds(pl.multiple_of(block * COLS + n * TILE, TILE), TILE)

    def copy(kind, index, src, dst, device):
        return pltpu.make_async_remote_copy(
            src_ref=src, dst_ref=dst, send_sem=send_sem.at[kind, index], recv_sem=recv_sem.at[kind, index],
            device_id=device, device_id_type=MESH,
        )

    def arrived(kind, index, where):
        copy(kind, index, where, where, to_sib).wait_recv()

    def sent(kind, index, where):
        copy(kind, index, where, where, to_sib).wait_send()

    barrier = pltpu.get_barrier_semaphore()
    for device in (to_right, to_left, {"tensor": across}, to_sib, to_anti, to_after, to_before):
        pl.semaphore_signal(barrier, inc=1, device_id=device, device_id_type=MESH)
    pl.semaphore_wait(barrier, 7)

    flag_self = flag_ref[d, s]
    flag_next = flag_ref[d, after]

    def quarter(k):
        return pl.ds(pl.multiple_of(k * TILE, TILE), TILE)

    for k in range(4):
        copy(W_ANTI, k, w_ref.at[:, quarter(k)], w_all.at[cols(d), quarter(k)], to_anti).start()
    copy(W_SIB, 0, w_ref, w_all.at[cols(d)], to_sib).start()
    for b in range(4):
        for k in range(1, 4):
            copy(
                X_ONE + k - 1, b, x_ref.at[:, :, cols(b)], x_all.at[b, :, t], {"tensor": lax.rem(t + k, 4)}
            ).start()
    loads = [pltpu.make_async_copy(x_ref.at[:, :, cols(b)], x_all.at[b, :, t], local_sem.at[b]) for b in range(4)]
    loads += [
        pltpu.make_async_copy(w_ref, w_all.at[cols(d)], local_sem.at[4]),
        pltpu.make_async_copy(cot_ref.at[:, :, cols(t)], cot.at[:, t], local_sem.at[5]),
    ]
    for load in loads:
        load.start()
    for k in range(1, 4):
        peer = lax.rem(t + k, 4)
        copy(C_COLS, k - 1, cot_ref.at[:, :, cols(peer)], cot.at[:, t], {"tensor": peer}).start()

    def normalize(read, j):
        def squares(b, total):
            u = read(b)
            u = u * u
            return total + (u[:, 0:128] + u[:, 128:256]) + (u[:, 256:384] + u[:, 384:512])

        total = lax.fori_loop(0, 8, squares, jnp.zeros((ROWS, 128), jnp.float32))
        inv = lax.rsqrt(jnp.sum(total, axis=-1, keepdims=True) * (1.0 / D) + EPSILON)

        def scale(b, _):
            where = pl.ds(pl.multiple_of(b * 512, 512), 512)
            nrm[j, :, :, where] = bf16(read(b) * inv * f32(gain_ref[:, where])).reshape(4, SLAB, 512)
            return 0

        lax.fori_loop(0, 8, scale, 0)
        return inv

    for b in range(4):
        loads[b].wait()
        for k in range(1, 4):
            arrived(X_ONE + k - 1, b, x_all.at[b, :, lax.rem(t + 4 - k, 4)])

    def first_norm(j, _):
        def read(b):
            where = pl.ds(pl.multiple_of(lax.rem(b, 2) * 512, 512), 512)
            return f32(x_all[b // 2, j, :, :, where]).reshape(ROWS, 512)

        normalize(read, j)
        return 0

    lax.fori_loop(0, CH, first_norm, 0)
    loads[4].wait()
    arrived(W_SIB, 0, w_all.at[cols(sib)])

    def add_rows(block, k, clear=False):
        there = quarter(k)
        product = jnp.dot(
            nrm[:, :, :, cols(block)].reshape(CH * ROWS, COLS), w_all[cols(block), there],
            preferred_element_type=jnp.float32,
        ).reshape(CH, ROWS, TILE)
        if clear:
            hid[:, :, there] = product
        else:
            hid[:, :, there] += product

    def turn_weight(k):
        def step(m, _):
            w_t[quarter(k), quarter(m)] = w_all[quarter(m), quarter(k)].T
            return 0

        lax.fori_loop(0, 16, step, 0)

    def first_tile(j, k):
        there = quarter(k)
        branch = f32(bf16(gelu(hid[j, :, there])))
        value = bf16(f32(x_all[t, j, :, :, there]).reshape(ROWS, TILE) + branch)
        y_cols[j, :, :, there] = value.reshape(4, SLAB, TILE)

    def take(k, _):
        add_rows(d, k, clear=True)
        add_rows(sib, k)
        theirs = w_all.at[cols(anti), quarter(k)]
        arrived(W_ANTI, k, theirs)
        copy(W_FWD, k, theirs, theirs, to_sib).start()
        add_rows(anti, k)
        arrived(W_FWD, k, w_all.at[cols(anti_sib), quarter(k)])
        add_rows(anti_sib, k)

        lax.fori_loop(0, CH, lambda j, _: (first_tile(j, k), 0)[1], 0)
        turn_weight(k)
        return 0

    def take_last(k):
        add_rows(d, k, clear=True)
        add_rows(sib, k)
        theirs = w_all.at[cols(anti), quarter(k)]
        arrived(W_ANTI, k, theirs)
        copy(W_FWD, k, theirs, theirs, to_sib).start()
        add_rows(anti, k)
        arrived(W_FWD, k, w_all.at[cols(anti_sib), quarter(k)])
        add_rows(anti_sib, k)

        def step(j, _):
            first_tile(j, k)
            copy(PRIOR_MOVE, j, y_cols.at[j], prior.at[j], to_after).start()
            return 0

        lax.fori_loop(0, CH, step, 0)
        turn_weight(k)

    lax.fori_loop(0, 3, take, 0)
    take_last(3)
    loads[5].wait()
    for k in range(1, 4):
        arrived(C_COLS, k - 1, cot.at[:, lax.rem(t + 4 - k, 4)])

    moments = [
        pltpu.make_async_copy(m1_ref, x_all.at[0:2], local_sem.at[0]),
        pltpu.make_async_copy(m2_ref, x_all.at[2:4], local_sem.at[1]),
    ]

    def choose(j):
        arrived(PRIOR_MOVE, j, prior.at[j])

        def step(n, _):
            there = quarter(n)
            mask = jnp.full((ROWS, TILE), flag_self, jnp.int32) == 1
            plain = f32(x_all[t, j, :, :, there]).reshape(ROWS, TILE)
            in_all[j, :, tile(t, n)] = bf16(jnp.where(mask, f32(prior[j, :, :, there]).reshape(ROWS, TILE), plain))
            return 0

        lax.fori_loop(0, 4, step, 0)
        mine = in_all.at[j, :, cols(t)]
        copy(GATHER_R, j, mine, mine, to_right).start()
        copy(GATHER_L, j, mine, mine, to_left).start()

        @pl.when(j == CH - 1)
        def _():
            for load in moments:
                load.start()

    def relay(j):
        arrived(GATHER_R, j, in_all.at[j, :, cols(left)])
        low = in_all.at[j, pl.ds(0, 64), cols(left)]
        copy(RELAY_R, j, low, low, to_right).start()
        arrived(GATHER_L, j, in_all.at[j, :, cols(right)])
        high = in_all.at[j, pl.ds(64, 64), cols(right)]
        copy(RELAY_L, j, high, high, to_left).start()

    def input_grad_tile(source, block, m, j, inv, slope):
        rows = tile(block, m)
        normed_grad = jnp.dot(source, w_t[:, rows], preferred_element_type=jnp.float32)
        return normed_grad * (inv * f32(gain_ref[:, rows])) - f32(in_all[j, :, rows]) * slope

    def forward(j):
        arrived(RELAY_R, j, in_all.at[j, pl.ds(0, 64), cols(across)])
        arrived(RELAY_L, j, in_all.at[j, pl.ds(64, 64), cols(across)])
        sent(PRIOR_MOVE, j, y_cols.at[j])
        inv = normalize(lambda b: f32(in_all[j, :, pl.ds(pl.multiple_of(b * 512, 512), 512)]), j)
        inv_s[j] = inv
        crossing = pl.ds(pl.multiple_of((1 - half) * 2048, 2048), 2048)
        copy(N_ANTI, j, nrm.at[j, t, :, crossing], n_anti.at[j, t], to_anti).start()
        copy(N_SIB, j, nrm.at[j, :, :, cols(sib)], n_sib.at[j], to_sib).start()

        def step(n, total):
            there = pl.ds(pl.multiple_of(n * TILE, TILE), TILE)
            hidden = jnp.dot(nrm[j].reshape(ROWS, D), w_all[:, there], preferred_element_type=jnp.float32)
            hid[j, :, there] = hidden
            branch = f32(bf16(gelu(hidden)))
            y_cols[j, :, :, there] = bf16(f32(in_all[j, :, tile(t, n)]) + branch).reshape(4, SLAB, TILE)
            upstream = f32(cot[j, :, :, there]).reshape(ROWS, TILE)
            grad = bf16(upstream * gelu_slope(hidden))
            hg[j, :, there] = grad
            return total + jnp.sum(f32(grad) * hidden, axis=-1, keepdims=True)

        total_s[j] = lax.fori_loop(0, 4, step, jnp.zeros((ROWS, 1), jnp.float32))

    def fill(target, block, j):
        inv = inv_s[j]
        slope = inv * inv * total_s[j] * (1.0 / D)

        def step(m, _):
            value = bf16(input_grad_tile(hg[j], block, m, j, inv, slope))
            target[j, :, quarter(m)] = value
            return 0

        lax.fori_loop(0, 4, step, 0)

    def far_sum(j):
        fill(opp, across, j)
        copy(OPP_R, j, opp.at[j, pl.ds(0, 64)], got_a.at[j], to_right).start()
        copy(OPP_L, j, opp.at[j, pl.ds(64, 64)], got_b.at[j], to_left).start()

    def near_sums(j):
        fill(to_r, right, j)
        fill(to_l, left, j)
        fill(own, t, j)

    def give_rows(j):
        for k in range(1, 4):
            peer = lax.rem(t + k, 4)
            copy(Y_ONE + k - 1, j, y_cols.at[j, peer], y_ref.at[j, :, cols(t)], {"tensor": peer}).start()
        pltpu.make_async_copy(y_cols.at[j, t], y_ref.at[j, :, cols(t)], local_sem.at[6 + j]).start()

    def add_halves(j):
        arrived(OPP_R, j, got_a.at[j])
        to_r[j, 0:64, :] = bf16(f32(to_r[j, 0:64, :]) + f32(got_a[j]))
        copy(SUM_R, j, to_r.at[j], got_l.at[j], to_right).start()
        arrived(OPP_L, j, got_b.at[j])
        to_l[j, 64:128, :] = bf16(f32(to_l[j, 64:128, :]) + f32(got_b[j]))
        copy(SUM_L, j, to_l.at[j], got_r.at[j], to_left).start()

    def carry_on(j):
        arrived(SUM_R, j, got_l.at[j])
        arrived(SUM_L, j, got_r.at[j])

        def step(n, _):
            there = pl.ds(pl.multiple_of(n * TILE, TILE), TILE)
            total = (f32(got_l[j, :, there]) + f32(got_r[j, :, there])) + f32(own[j, :, there])
            own[j, :, there] = bf16(f32(cot[j, :, :, there]).reshape(ROWS, TILE) + total)
            return 0

        lax.fori_loop(0, 4, step, 0)
        copy(CARRY_MOVE, j, own.at[j], incoming.at[j], to_before).start()

    def backward(j):
        arrived(CARRY_MOVE, j, incoming.at[j])

        def step(n, total):
            there = pl.ds(pl.multiple_of(n * TILE, TILE), TILE)
            mask = jnp.full((ROWS, TILE), flag_next, jnp.int32) == 1
            upstream = f32(cot[j, :, :, there]).reshape(ROWS, TILE)
            summed = bf16(upstream + jnp.where(mask, f32(incoming[j, :, there]), 0.0))
            incoming[j, :, there] = summed
            hidden = hid[j, :, there]
            grad = bf16(f32(summed) * gelu_slope(hidden))
            hg[j, :, there] = grad
            return total + jnp.sum(f32(grad) * hidden, axis=-1, keepdims=True)

        total_s[j] = lax.fori_loop(0, 4, step, jnp.zeros((ROWS, 1), jnp.float32))
        copy(HG_ANTI, j, hg.at[j], hg_anti.at[j], to_anti).start()
        copy(HG_SIB, j, hg.at[j], hg_sib.at[j], to_sib).start()

    def row_sums(j):
        inv = inv_s[j]
        slope = inv * inv * total_s[j] * (1.0 / D)

        def other(q, _):
            block = lax.rem(t + 1 + q // 4, 4)
            m = lax.rem(q, 4)
            value = bf16(input_grad_tile(hg[j], block, m, j, inv, slope))
            part[j, :, :, tile(block, m)] = value.reshape(4, SLAB, TILE)
            return 0

        lax.fori_loop(0, 12, other, 0)

        def mine(m, _):
            there = pl.ds(pl.multiple_of(m * TILE, TILE), TILE)
            value = input_grad_tile(hg[j], t, m, j, inv, slope) + f32(incoming[j, :, there])
            part[j, :, :, tile(t, m)] = bf16(value).reshape(4, SLAB, TILE)
            return 0

        lax.fori_loop(0, 4, mine, 0)
        copy(ROW_OPP_R, j, part.at[j, across, pl.ds(0, 16)], row_a.at[j], to_right).start()
        copy(ROW_OPP_L, j, part.at[j, across, pl.ds(16, 16)], row_b.at[j], to_left).start()

    def add_row_halves(j):
        arrived(ROW_OPP_R, j, row_a.at[j])
        part[j, right, 0:16, :] = bf16(f32(part[j, right, 0:16, :]) + f32(row_a[j]))
        copy(ROW_SUM_R, j, part.at[j, right], row_l.at[j], to_right).start()
        arrived(ROW_OPP_L, j, row_b.at[j])
        part[j, left, 16:32, :] = bf16(f32(part[j, left, 16:32, :]) + f32(row_b[j]))
        copy(ROW_SUM_L, j, part.at[j, left], row_r.at[j], to_left).start()

    def finish_rows(j):
        arrived(ROW_SUM_R, j, row_l.at[j])
        arrived(ROW_SUM_L, j, row_r.at[j])

        def step(b, _):
            there = pl.ds(pl.multiple_of(b * 1024, 1024), 1024)
            total = (f32(row_l[j, :, there]) + f32(row_r[j, :, there])) + f32(part[j, t, :, there])
            mask = jnp.full((SLAB, 1024), flag_self, jnp.int32) == 1
            row_l[j, :, there] = bf16(jnp.where(mask, 0.0, total))
            return 0

        lax.fori_loop(0, 4, step, 0)
        pltpu.make_async_copy(row_l.at[j], dx_ref.at[j], local_sem.at[10 + j]).start()

    def spread_normed(j):
        arrived(N_ANTI, j, n_anti.at[j, t])
        copy(N_R, j, n_anti.at[j, t], n_anti.at[j, t], to_right).start()
        copy(N_L, j, n_anti.at[j, t], n_anti.at[j, t], to_left).start()

    def relay_normed(j):
        arrived(N_R, j, n_anti.at[j, left])
        low = n_anti.at[j, left, pl.ds(0, 16)]
        copy(N_RELAY_R, j, low, low, to_right).start()
        arrived(N_L, j, n_anti.at[j, right])
        high = n_anti.at[j, right, pl.ds(16, 16)]
        copy(N_RELAY_L, j, high, high, to_left).start()

    def share_normed(j):
        arrived(N_RELAY_R, j, n_anti.at[j, across, pl.ds(0, 16)])
        arrived(N_RELAY_L, j, n_anti.at[j, across, pl.ds(16, 16)])
        theirs = pl.ds(pl.multiple_of((1 - core) * COLS, COLS), COLS)
        copy(N_SHARE, j, n_anti.at[j, :, :, theirs], n_other.at[j], to_sib).start()

    def pass_grad(j):
        arrived(HG_ANTI, j, hg_anti.at[j])
        copy(HG_FWD, j, hg_anti.at[j], hg_other.at[j], to_sib).start()

    def stage(run, j):
        pl.when(jnp.logical_and(j >= 0, j < CH))(lambda: run(j))

    def turn(i, _):
        stage(relay_normed, i - 4)
        stage(choose, i)
        stage(near_sums, i - 3)
        stage(share_normed, i - 6)
        stage(relay, i - 1)
        stage(forward, i - 2)
        stage(pass_grad, i - 8)
        stage(carry_on, i - 4)
        stage(spread_normed, i - 3)
        stage(add_halves, i - 3)
        stage(backward, i - 5)
        stage(give_rows, i - 10)
        stage(far_sum, i - 2)
        stage(row_sums, i - 5)
        stage(add_row_halves, i - 6)
        stage(finish_rows, i - 9)
        return 0

    lax.fori_loop(0, CH + 10, turn, 0)

    def last_arrivals(j, _):
        arrived(HG_SIB, j, hg_sib.at[j])
        arrived(HG_FWD, j, hg_other.at[j])
        arrived(N_SIB, j, n_sib.at[j])
        arrived(N_SHARE, j, n_other.at[j])
        return 0

    lax.fori_loop(0, CH, last_arrivals, 0)
    for load in moments:
        load.wait()

    def product(left_rows, right_rows):
        return lax.dot_general(
            left_rows.reshape(CH * ROWS, TILE), right_rows.reshape(CH * ROWS, 512),
            (((0,), (0,)), ((), ())), preferred_element_type=jnp.float32,
        )

    def step_dir(q, _):
        f = q // 2
        rows = pl.ds(pl.multiple_of(f * TILE, TILE), TILE)
        there = pl.ds(pl.multiple_of(lax.rem(q, 2) * 512, 512), 512)
        total = product(nrm[:, :, :, tile(d, f)], hg[:, :, there])
        total += product(n_sib[:, :, :, rows], hg_sib[:, :, there])
        total += product(n_anti[:, :, :, tile(core, f)], hg_anti[:, :, there])
        total += product(n_other[:, :, :, rows], hg_other[:, :, there])
        total = total * (1.0 / (4 * CH * ROWS))
        pair = pl.ds(lax.rem(f, 2) * 2, 2)
        one = f32(x_all[f // 2, pair, :, :, there]).reshape(TILE, 512)
        two = f32(x_all[2 + f // 2, pair, :, :, there]).reshape(TILE, 512)
        first = BETA_ONE * one + (1.0 - BETA_ONE) * total
        second = BETA_TWO * two + (1.0 - BETA_TWO) * total * total
        value = bf16(first / (jnp.sqrt(second) + 1e-08))
        x_all[f // 2, pair, :, :, there] = value.reshape(2, 4, SLAB, 512)
        return 0

    lax.fori_loop(0, 8, step_dir, 0)
    out = pltpu.make_async_copy(x_all.at[0:2], upd_ref, local_sem.at[14])
    out.start()

    def drain(j, _):
        for k in range(1, 4):
            arrived(Y_ONE + k - 1, j, y_ref.at[j, :, cols(lax.rem(t + 4 - k, 4))])
            sent(Y_ONE + k - 1, j, y_cols.at[j, 0])
        pltpu.make_async_copy(y_cols.at[j, t], y_ref.at[j, :, cols(t)], local_sem.at[6 + j]).wait()
        pltpu.make_async_copy(row_l.at[j], dx_ref.at[j], local_sem.at[10 + j]).wait()
        sent(W_ANTI, j, w_all.at[cols(d), quarter(j)])
        sent(W_FWD, j, w_all.at[cols(anti), quarter(j)])
        for q in range(3):
            sent(X_ONE + q, j, x_all.at[j, :, t])
        sent(GATHER_R, j, in_all.at[j, :, cols(t)])
        sent(GATHER_L, j, in_all.at[j, :, cols(t)])
        sent(RELAY_R, j, in_all.at[j, pl.ds(0, 64), cols(left)])
        sent(RELAY_L, j, in_all.at[j, pl.ds(64, 64), cols(right)])
        sent(OPP_R, j, opp.at[j, pl.ds(0, 64)])
        sent(OPP_L, j, opp.at[j, pl.ds(64, 64)])
        sent(SUM_R, j, to_r.at[j])
        sent(SUM_L, j, to_l.at[j])
        sent(CARRY_MOVE, j, own.at[j])
        sent(ROW_OPP_R, j, part.at[j, across, pl.ds(0, 16)])
        sent(ROW_OPP_L, j, part.at[j, across, pl.ds(16, 16)])
        sent(ROW_SUM_R, j, part.at[j, right])
        sent(ROW_SUM_L, j, part.at[j, left])
        sent(HG_SIB, j, hg.at[j])
        sent(HG_ANTI, j, hg.at[j])
        sent(HG_FWD, j, hg_anti.at[j])
        sent(N_ANTI, j, n_anti.at[j, t])
        sent(N_SIB, j, n_sib.at[j])
        sent(N_R, j, n_anti.at[j, t])
        sent(N_L, j, n_anti.at[j, t])
        sent(N_RELAY_R, j, n_anti.at[j, left, pl.ds(0, 16)])
        sent(N_RELAY_L, j, n_anti.at[j, right, pl.ds(16, 16)])
        sent(N_SHARE, j, n_other.at[j])
        return 0

    lax.fori_loop(0, CH, drain, 0)
    sent(W_SIB, 0, w_all.at[cols(d)])
    for k in range(3):
        sent(C_COLS, k, cot.at[:, t])
    out.wait()


def whole(x, cot, w, m1, m2, gain, flags):
    def vm(*shape, dtype=jnp.bfloat16):
        return pltpu.VMEM(shape, dtype)

    scratch = [
        vm(D, COLS), vm(COLS, D), vm(4, CH, 4, SLAB, COLS), vm(CH, ROWS, D), vm(CH, 4, SLAB, D),
        vm(CH, ROWS, COLS, dtype=jnp.float32), vm(CH, 4, SLAB, COLS),
        vm(CH, 4, SLAB, COLS), vm(CH, ROWS, COLS), vm(CH, 4, SLAB, COLS),
        vm(CH, ROWS, COLS), vm(CH, ROWS, COLS), vm(CH, ROWS, COLS), vm(CH, ROWS, COLS),
        vm(CH, 64, COLS), vm(CH, 64, COLS), vm(CH, ROWS, COLS), vm(CH, ROWS, COLS),
        vm(CH, 4, SLAB, D), vm(CH, 16, D), vm(CH, 16, D), vm(CH, SLAB, D), vm(CH, SLAB, D),
        vm(CH, ROWS, COLS), vm(CH, ROWS, COLS), vm(CH, ROWS, COLS), vm(CH, ROWS, COLS),
        vm(CH, 4, SLAB, COLS), vm(CH, 4, SLAB, 2 * COLS), vm(CH, 4, SLAB, COLS),
        vm(CH, ROWS, 1, dtype=jnp.float32), vm(CH, ROWS, 1, dtype=jnp.float32),
        pltpu.SemaphoreType.DMA((34, CH)), pltpu.SemaphoreType.DMA((34, CH)), pltpu.SemaphoreType.DMA((15,)),
    ]
    anywhere = pl.BlockSpec(memory_space=pl.ANY)
    near = pl.BlockSpec(memory_space=pltpu.VMEM)
    return pl.pallas_call(
        kernel,
        out_shape=(
            jax.ShapeDtypeStruct((CH, SLAB, D), jnp.bfloat16),
            jax.ShapeDtypeStruct((CH, SLAB, D), jnp.bfloat16),
            jax.ShapeDtypeStruct((2, 4, 4, SLAB, COLS), jnp.bfloat16),
        ),
        in_specs=[anywhere] * 5 + [near, pl.BlockSpec(memory_space=pltpu.SMEM)],
        out_specs=(anywhere,) * 3,
        scratch_shapes=scratch,
        compiler_params=pltpu.CompilerParams(
            collective_id=0, has_side_effects=True, vmem_limit_bytes=63 * 2**20
        ),
        cost_estimate=pl.CostEstimate(flops=21 * 10**9, bytes_accessed=20 * 2**20, transcendentals=2 * 10**6),
    )(x, cot, w, m1, m2, gain, flags)


def body(x_in, gain, weight, moment_one, moment_two, cotangent, preempted):
    y, dx, update = whole(
        x_in.reshape(CH, SLAB, D), cotangent.reshape(CH, SLAB, D), weight[0],
        moment_one.reshape(2, 4, 4, SLAB, COLS), moment_two.reshape(2, 4, 4, SLAB, COLS), gain, preempted,
    )
    return (y.reshape(1, CH * SLAB, D), dx.reshape(1, CH * SLAB, D), update.reshape(1, COLS, COLS))


def solution(mesh):
    placed = (
        P("section", ("dp", "tensor"), None),
        P("section", None),
        P("section", "dp", "tensor"),
        P("section", "dp", "tensor"),
        P("section", "dp", "tensor"),
        P("section", ("dp", "tensor"), None),
        P(),
    )
    return jax.shard_map(
        body,
        mesh=mesh,
        in_specs=placed,
        out_specs=(
            P("section", ("dp", "tensor"), None),
            P("section", ("dp", "tensor"), None),
            P("section", "dp", "tensor"),
        ),
        check_vma=False,
    )
```

time: 298 us -> 275 us (0.923)
  the two profiles are of different devices: /device:TPU:1 before, /device:TPU:191 now
where the time goes in v3:
time: 275 us
  Pallas kernels  270 us (98%)
  local copies, waits for them, and re-layouts  4.74 us (2%)
    pallas_call x1, Pallas kernels, whole(): pl.pallas_call(kernel, out_shape=(jax.ShapeDtypeStruct((CH, SLAB, D), jnp...  270 us

profile of v3, /device:TPU:191, one launch (start us, length us, event | category | flops | bytes accessed | tf_op | source)
XLA Modules:
  0.0 274.9 jit_solution(17935426682816240181)
XLA Ops:
  0.6 269.5 %shard_map.94 = (bf16[4,32,4096]{2,1,0:T(8,128)(2,1)}, bf16[4,32,4096]{2,1,0:T(8,128)(2,1)}, bf16[2,4,4,32,1024]{4,3,2,1,0:T(8,128)(2,1)}) custom-call(bf16[4,32,4096]{2,1,0:T(8,128)(2,1)} %bitcast.14, bf16[4,32,4096]{2,1,0:T(8,128)(2,1)} %bitcast.15, bf16[1024,1024]{1,0:T(8,128)(2,1)} %bitcast.11, bf16[2,4,4,32,1024]{4,3,2,1,0:T(8,128)(2,1)} %bitcast.12, ...), custom_call_target="tpu_custom_call" | custom-call | flops 20999999488 | bytes 20971520 | tf_op jit(solution)/shard_map/pallas_call | solution.py:532
  270.2 0.0 copy-start.1
  270.2 0.0 copy-start
  270.2 2.4 copy.13
  272.6 0.0 copy-done.1
  272.6 1.0 copy.14
  273.6 0.0 copy-done
  273.6 1.3 copy.15
Async XLA Ops:
  270.2 2.5 copy-start.1
  270.2 3.4 %copy-start = (bf16[2,4,4,32,1024]{4,3,2,1,0:T(8,128)(2,1)S(1)}, bf16[2,4,4,32,1024]{4,3,2,1,0:T(8,128)(2,1)}, u32[]{:S(2)}) copy-start(bf16[2,4,4,32,1024]{4,3,2,1,0:T(8,128)(2,1)} %get-tuple-element.8) | copy-start | bytes 6291460

commit v4 on v3

--- a/solution.py
+++ b/solution.py
@@ -255,9 +255,6 @@
         sent(PRIOR_MOVE, j, y_cols.at[j])
         inv = normalize(lambda b: f32(in_all[j, :, pl.ds(pl.multiple_of(b * 512, 512), 512)]), j)
         inv_s[j] = inv
-        crossing = pl.ds(pl.multiple_of((1 - half) * 2048, 2048), 2048)
-        copy(N_ANTI, j, nrm.at[j, t, :, crossing], n_anti.at[j, t], to_anti).start()
-        copy(N_SIB, j, nrm.at[j, :, :, cols(sib)], n_sib.at[j], to_sib).start()
 
         def step(n, total):
             there = pl.ds(pl.multiple_of(n * TILE, TILE), TILE)
@@ -272,6 +269,11 @@
 
         total_s[j] = lax.fori_loop(0, 4, step, jnp.zeros((ROWS, 1), jnp.float32))
 
+    def send_normed(j):
+        crossing = pl.ds(pl.multiple_of((1 - half) * 2048, 2048), 2048)
+        copy(N_ANTI, j, nrm.at[j, t, :, crossing], n_anti.at[j, t], to_anti).start()
+        copy(N_SIB, j, nrm.at[j, :, :, cols(sib)], n_sib.at[j], to_sib).start()
+
     def fill(target, block, j):
         inv = inv_s[j]
         slope = inv * inv * total_s[j] * (1.0 / D)
@@ -335,6 +337,8 @@
             return total + jnp.sum(f32(grad) * hidden, axis=-1, keepdims=True)
 
         total_s[j] = lax.fori_loop(0, 4, step, jnp.zeros((ROWS, 1), jnp.float32))
+
+    def send_grads(j):
         copy(HG_ANTI, j, hg.at[j], hg_anti.at[j], to_anti).start()
         copy(HG_SIB, j, hg.at[j], hg_sib.at[j], to_sib).start()
 
@@ -410,25 +414,26 @@
         pl.when(jnp.logical_and(j >= 0, j < CH))(lambda: run(j))
 
     def turn(i, _):
-        stage(relay_normed, i - 4)
+        stage(carry_on, i - 6)
+        stage(give_rows, i - 7)
+        stage(pass_grad, i - 19)
+        stage(relay_normed, i - 9)
         stage(choose, i)
+        stage(spread_normed, i - 6)
+        stage(relay, i - 1)
+        stage(backward, i - 7)
+        stage(far_sum, i - 3)
+        stage(send_grads, i - 7)
+        stage(forward, i - 2)
+        stage(add_row_halves, i - 10)
+        stage(row_sums, i - 7)
+        stage(send_normed, i - 2)
         stage(near_sums, i - 3)
-        stage(share_normed, i - 6)
-        stage(relay, i - 1)
-        stage(forward, i - 2)
-        stage(pass_grad, i - 8)
-        stage(carry_on, i - 4)
-        stage(spread_normed, i - 3)
-        stage(add_halves, i - 3)
-        stage(backward, i - 5)
-        stage(give_rows, i - 10)
-        stage(far_sum, i - 2)
-        stage(row_sums, i - 5)
-        stage(add_row_halves, i - 6)
-        stage(finish_rows, i - 9)
+        stage(add_halves, i - 4)
+        stage(share_normed, i - 18)
         return 0
 
-    lax.fori_loop(0, CH + 10, turn, 0)
+    lax.fori_loop(0, CH + 19, turn, 0)
 
     def last_arrivals(j, _):
         arrived(HG_SIB, j, hg_sib.at[j])
@@ -468,6 +473,7 @@
     lax.fori_loop(0, 8, step_dir, 0)
     out = pltpu.make_async_copy(x_all.at[0:2], upd_ref, local_sem.at[14])
     out.start()
+    lax.fori_loop(0, CH, lambda j, _: (finish_rows(j), 0)[1], 0)
 
     def drain(j, _):
         for k in range(1, 4):

time: 275 us -> 262 us (0.953)
  the two profiles are of different devices: /device:TPU:191 before, /device:TPU:1 now
where the time goes in v4:
time: 262 us
  Pallas kernels  256 us (98%)
  local copies, waits for them, and re-layouts  4.74 us (2%)
    pallas_call x1, Pallas kernels, whole(): pl.pallas_call(kernel, out_shape=(jax.ShapeDtypeStruct((CH, SLAB, D), jnp...  256 us

profile of v4, /device:TPU:1, one launch (start us, length us, event | category | flops | bytes accessed | tf_op | source)
XLA Modules:
  0.0 261.7 jit_solution(15577443789705807544)
XLA Ops:
  0.6 256.3 %shard_map.94 = (bf16[4,32,4096]{2,1,0:T(8,128)(2,1)}, bf16[4,32,4096]{2,1,0:T(8,128)(2,1)}, bf16[2,4,4,32,1024]{4,3,2,1,0:T(8,128)(2,1)}) custom-call(bf16[4,32,4096]{2,1,0:T(8,128)(2,1)} %bitcast.14, bf16[4,32,4096]{2,1,0:T(8,128)(2,1)} %bitcast.15, bf16[1024,1024]{1,0:T(8,128)(2,1)} %bitcast.11, bf16[2,4,4,32,1024]{4,3,2,1,0:T(8,128)(2,1)} %bitcast.12, ...), custom_call_target="tpu_custom_call" | custom-call | flops 20999999488 | bytes 20971520 | tf_op jit(solution)/shard_map/pallas_call | solution.py:538
  256.9 0.0 copy-start.1
  256.9 0.0 copy-start
  256.9 2.4 copy.13
  259.4 0.0 copy-done.1
  259.4 1.0 copy.14
  260.3 0.0 copy-done
  260.3 1.3 copy.15
Async XLA Ops:
  256.9 2.5 copy-start.1
  256.9 3.4 %copy-start = (bf16[2,4,4,32,1024]{4,3,2,1,0:T(8,128)(2,1)S(1)}, bf16[2,4,4,32,1024]{4,3,2,1,0:T(8,128)(2,1)}, u32[]{:S(2)}) copy-start(bf16[2,4,4,32,1024]{4,3,2,1,0:T(8,128)(2,1)} %get-tuple-element.8) | copy-start | bytes 6291460

commit v5 on v4

--- a/solution.py
+++ b/solution.py
@@ -19,10 +19,10 @@
 TILE = 256
 MESH = pl.DeviceIdType.MESH
 
-(W_ANTI, W_FWD, W_SIB, X_ONE, X_TWO, X_THREE, C_COLS, PRIOR_MOVE, GATHER_R, GATHER_L, RELAY_R, RELAY_L,
+(W_ANTI, W_FWD, W_SIB, X_ONE, X_TWO, X_THREE, C_COLS, PRIOR_MOVE, PRIOR_HIGH, HIGH_R, LOW_L, GATHER_R, GATHER_L, RELAY_R, RELAY_L,
  Y_ONE, Y_TWO, Y_THREE,
  OPP_R, OPP_L, SUM_R, SUM_L, CARRY_MOVE, ROW_OPP_R, ROW_OPP_L, ROW_SUM_R, ROW_SUM_L, HG_SIB, HG_ANTI, HG_FWD,
- N_ANTI, N_SIB, N_R, N_L, N_RELAY_R, N_RELAY_L, N_SHARE) = range(34)
+ N_ANTI, N_SIB, N_R, N_L, N_RELAY_R, N_RELAY_L, N_SHARE) = range(37)
 
 
 def gelu(v):
@@ -199,7 +199,8 @@
 
         def step(j, _):
             first_tile(j, k)
-            copy(PRIOR_MOVE, j, y_cols.at[j], prior.at[j], to_after).start()
+            for kind, part_of in ((PRIOR_MOVE, pl.ds(0, 2)), (PRIOR_HIGH, pl.ds(2, 2))):
+                copy(kind, j, y_cols.at[j, part_of], prior.at[j, part_of], to_after).start()
             return 0
 
         lax.fori_loop(0, CH, step, 0)
@@ -216,20 +217,27 @@
         pltpu.make_async_copy(m2_ref, x_all.at[2:4], local_sem.at[1]),
     ]
 
-    def choose(j):
-        arrived(PRIOR_MOVE, j, prior.at[j])
+    def choose_half(j, h):
+        slabs, rows = pl.ds(2 * h, 2), pl.ds(64 * h, 64)
 
         def step(n, _):
             there = quarter(n)
-            mask = jnp.full((ROWS, TILE), flag_self, jnp.int32) == 1
-            plain = f32(x_all[t, j, :, :, there]).reshape(ROWS, TILE)
-            in_all[j, :, tile(t, n)] = bf16(jnp.where(mask, f32(prior[j, :, :, there]).reshape(ROWS, TILE), plain))
+            mask = jnp.full((64, TILE), flag_self, jnp.int32) == 1
+            plain = f32(x_all[t, j, slabs, :, there]).reshape(64, TILE)
+            value = bf16(jnp.where(mask, f32(prior[j, slabs, :, there]).reshape(64, TILE), plain))
+            in_all[j, rows, tile(t, n)] = value
             return 0
 
         lax.fori_loop(0, 4, step, 0)
-        mine = in_all.at[j, :, cols(t)]
-        copy(GATHER_R, j, mine, mine, to_right).start()
-        copy(GATHER_L, j, mine, mine, to_left).start()
+        mine = in_all.at[j, rows, cols(t)]
+        copy(HIGH_R if h else GATHER_R, j, mine, mine, to_right).start()
+        copy(GATHER_L if h else LOW_L, j, mine, mine, to_left).start()
+
+    def choose(j):
+        arrived(PRIOR_MOVE, j, prior.at[j, pl.ds(0, 2)])
+        choose_half(j, 0)
+        arrived(PRIOR_HIGH, j, prior.at[j, pl.ds(2, 2)])
+        choose_half(j, 1)
 
         @pl.when(j == CH - 1)
         def _():
@@ -237,10 +245,10 @@
                 load.start()
 
     def relay(j):
-        arrived(GATHER_R, j, in_all.at[j, :, cols(left)])
+        arrived(GATHER_R, j, in_all.at[j, pl.ds(0, 64), cols(left)])
         low = in_all.at[j, pl.ds(0, 64), cols(left)]
         copy(RELAY_R, j, low, low, to_right).start()
-        arrived(GATHER_L, j, in_all.at[j, :, cols(right)])
+        arrived(GATHER_L, j, in_all.at[j, pl.ds(64, 64), cols(right)])
         high = in_all.at[j, pl.ds(64, 64), cols(right)]
         copy(RELAY_L, j, high, high, to_left).start()
 
@@ -252,7 +260,10 @@
     def forward(j):
         arrived(RELAY_R, j, in_all.at[j, pl.ds(0, 64), cols(across)])
         arrived(RELAY_L, j, in_all.at[j, pl.ds(64, 64), cols(across)])
-        sent(PRIOR_MOVE, j, y_cols.at[j])
+        arrived(HIGH_R, j, in_all.at[j, pl.ds(64, 64), cols(left)])
+        arrived(LOW_L, j, in_all.at[j, pl.ds(0, 64), cols(right)])
+        sent(PRIOR_MOVE, j, y_cols.at[j, pl.ds(0, 2)])
+        sent(PRIOR_HIGH, j, y_cols.at[j, pl.ds(2, 2)])
         inv = normalize(lambda b: f32(in_all[j, :, pl.ds(pl.multiple_of(b * 512, 512), 512)]), j)
         inv_s[j] = inv
 
@@ -485,8 +496,10 @@
         sent(W_FWD, j, w_all.at[cols(anti), quarter(j)])
         for q in range(3):
             sent(X_ONE + q, j, x_all.at[j, :, t])
-        sent(GATHER_R, j, in_all.at[j, :, cols(t)])
-        sent(GATHER_L, j, in_all.at[j, :, cols(t)])
+        sent(GATHER_R, j, in_all.at[j, pl.ds(0, 64), cols(t)])
+        sent(HIGH_R, j, in_all.at[j, pl.ds(64, 64), cols(t)])
+        sent(LOW_L, j, in_all.at[j, pl.ds(0, 64), cols(t)])
+        sent(GATHER_L, j, in_all.at[j, pl.ds(64, 64), cols(t)])
         sent(RELAY_R, j, in_all.at[j, pl.ds(0, 64), cols(left)])
         sent(RELAY_L, j, in_all.at[j, pl.ds(64, 64), cols(right)])
         sent(OPP_R, j, opp.at[j, pl.ds(0, 64)])
@@ -531,7 +544,7 @@
         vm(CH, ROWS, COLS), vm(CH, ROWS, COLS), vm(CH, ROWS, COLS), vm(CH, ROWS, COLS),
         vm(CH, 4, SLAB, COLS), vm(CH, 4, SLAB, 2 * COLS), vm(CH, 4, SLAB, COLS),
         vm(CH, ROWS, 1, dtype=jnp.float32), vm(CH, ROWS, 1, dtype=jnp.float32),
-        pltpu.SemaphoreType.DMA((34, CH)), pltpu.SemaphoreType.DMA((34, CH)), pltpu.SemaphoreType.DMA((15,)),
+        pltpu.SemaphoreType.DMA((37, CH)), pltpu.SemaphoreType.DMA((37, CH)), pltpu.SemaphoreType.DMA((15,)),
     ]
     anywhere = pl.BlockSpec(memory_space=pl.ANY)
     near = pl.BlockSpec(memory_space=pltpu.VMEM)

time: 262 us -> 259 us (0.989)
  no operation moved by 1% of the time
where the time goes in v5:
time: 259 us
  Pallas kernels  254 us (98%)
  local copies, waits for them, and re-layouts  4.74 us (2%)
    pallas_call x1, Pallas kernels, whole(): pl.pallas_call(kernel, out_shape=(jax.ShapeDtypeStruct((CH, SLAB, D), jnp...  254 us

profile of v5, /device:TPU:1, one launch (start us, length us, event | category | flops | bytes accessed | tf_op | source)
XLA Modules:
  0.0 259.1 jit_solution(15231753753080696285)
XLA Ops:
  0.6 253.7 %shard_map.94 = (bf16[4,32,4096]{2,1,0:T(8,128)(2,1)}, bf16[4,32,4096]{2,1,0:T(8,128)(2,1)}, bf16[2,4,4,32,1024]{4,3,2,1,0:T(8,128)(2,1)}) custom-call(bf16[4,32,4096]{2,1,0:T(8,128)(2,1)} %bitcast.14, bf16[4,32,4096]{2,1,0:T(8,128)(2,1)} %bitcast.15, bf16[1024,1024]{1,0:T(8,128)(2,1)} %bitcast.11, bf16[2,4,4,32,1024]{4,3,2,1,0:T(8,128)(2,1)} %bitcast.12, ...), custom_call_target="tpu_custom_call" | custom-call | flops 20999999488 | bytes 20971520 | tf_op jit(solution)/shard_map/pallas_call | solution.py:551
  254.3 0.0 copy-start.1
  254.3 0.0 copy-start
  254.3 2.4 copy.13
  256.8 0.0 copy-done.1
  256.8 1.0 copy.14
  257.7 0.0 copy-done
  257.7 1.3 copy.15
Async XLA Ops:
  254.3 2.5 copy-start.1
  254.3 3.4 %copy-start = (bf16[2,4,4,32,1024]{4,3,2,1,0:T(8,128)(2,1)S(1)}, bf16[2,4,4,32,1024]{4,3,2,1,0:T(8,128)(2,1)}, u32[]{:S(2)}) copy-start(bf16[2,4,4,32,1024]{4,3,2,1,0:T(8,128)(2,1)} %get-tuple-element.8) | copy-start | bytes 6291460

commit v6 on v5

--- a/solution.py
+++ b/solution.py
@@ -96,8 +96,11 @@
     def quarter(k):
         return pl.ds(pl.multiple_of(k * TILE, TILE), TILE)
 
-    for k in range(4):
+    pieces = ((W_ANTI, W_FWD, 3, 3, pl.ds(768, 128)), (W_SIB, W_SIB, 1, 2, pl.ds(896, 128)))
+    for k in range(3):
         copy(W_ANTI, k, w_ref.at[:, quarter(k)], w_all.at[cols(d), quarter(k)], to_anti).start()
+    for kind, _, index, _, there in pieces:
+        copy(kind, index, w_ref.at[:, there], w_all.at[cols(d), there], to_anti).start()
     copy(W_SIB, 0, w_ref, w_all.at[cols(d)], to_sib).start()
     for b in range(4):
         for k in range(1, 4):
@@ -190,11 +193,13 @@
     def take_last(k):
         add_rows(d, k, clear=True)
         add_rows(sib, k)
-        theirs = w_all.at[cols(anti), quarter(k)]
-        arrived(W_ANTI, k, theirs)
-        copy(W_FWD, k, theirs, theirs, to_sib).start()
+        for kind, onward, index, at, there in pieces:
+            theirs = w_all.at[cols(anti), there]
+            arrived(kind, index, theirs)
+            copy(onward, at, theirs, theirs, to_sib).start()
         add_rows(anti, k)
-        arrived(W_FWD, k, w_all.at[cols(anti_sib), quarter(k)])
+        for _, onward, _, at, there in pieces:
+            arrived(onward, at, w_all.at[cols(anti_sib), there])
         add_rows(anti_sib, k)
 
         def step(j, _):
@@ -492,8 +497,6 @@
             sent(Y_ONE + k - 1, j, y_cols.at[j, 0])
         pltpu.make_async_copy(y_cols.at[j, t], y_ref.at[j, :, cols(t)], local_sem.at[6 + j]).wait()
         pltpu.make_async_copy(row_l.at[j], dx_ref.at[j], local_sem.at[10 + j]).wait()
-        sent(W_ANTI, j, w_all.at[cols(d), quarter(j)])
-        sent(W_FWD, j, w_all.at[cols(anti), quarter(j)])
         for q in range(3):
             sent(X_ONE + q, j, x_all.at[j, :, t])
         sent(GATHER_R, j, in_all.at[j, pl.ds(0, 64), cols(t)])
@@ -527,6 +530,11 @@
     sent(W_SIB, 0, w_all.at[cols(d)])
     for k in range(3):
         sent(C_COLS, k, cot.at[:, t])
+        sent(W_ANTI, k, w_all.at[cols(d), quarter(k)])
+        sent(W_FWD, k, w_all.at[cols(anti), quarter(k)])
+    for kind, onward, index, at, there in pieces:
+        sent(kind, index, w_all.at[cols(d), there])
+        sent(onward, at, w_all.at[cols(anti), there])
     out.wait()
 
 

time: 259 us -> 261 us (level)
  no operation moved by 1% of the time
where the time goes in v6:
time: 261 us
  Pallas kernels  256 us (98%)
  local copies, waits for them, and re-layouts  4.74 us (2%)
    pallas_call x1, Pallas kernels, whole(): pl.pallas_call(kernel, out_shape=(jax.ShapeDtypeStruct((CH, SLAB, D), jnp...  256 us

profile of v6, /device:TPU:1, one launch (start us, length us, event | category | flops | bytes accessed | tf_op | source)
XLA Modules:
  0.0 261.1 jit_solution(13977019793821857696)
XLA Ops:
  0.6 255.8 %shard_map.94 = (bf16[4,32,4096]{2,1,0:T(8,128)(2,1)}, bf16[4,32,4096]{2,1,0:T(8,128)(2,1)}, bf16[2,4,4,32,1024]{4,3,2,1,0:T(8,128)(2,1)}) custom-call(bf16[4,32,4096]{2,1,0:T(8,128)(2,1)} %bitcast.14, bf16[4,32,4096]{2,1,0:T(8,128)(2,1)} %bitcast.15, bf16[1024,1024]{1,0:T(8,128)(2,1)} %bitcast.11, bf16[2,4,4,32,1024]{4,3,2,1,0:T(8,128)(2,1)} %bitcast.12, ...), custom_call_target="tpu_custom_call" | custom-call | flops 20999999488 | bytes 20971520 | tf_op jit(solution)/shard_map/pallas_call | solution.py:559
  256.4 0.0 copy-start.1
  256.4 0.0 copy-start
  256.4 2.4 copy.13
  258.9 0.0 copy-done.1
  258.9 1.0 copy.14
  259.8 0.0 copy-done
  259.8 1.3 copy.15
Async XLA Ops:
  256.4 2.5 copy-start.1
  256.4 3.4 %copy-start = (bf16[2,4,4,32,1024]{4,3,2,1,0:T(8,128)(2,1)S(1)}, bf16[2,4,4,32,1024]{4,3,2,1,0:T(8,128)(2,1)}, u32[]{:S(2)}) copy-start(bf16[2,4,4,32,1024]{4,3,2,1,0:T(8,128)(2,1)} %get-tuple-element.8) | copy-start | bytes 6291460
